TPU v7x, 128 devices: a whole 4x4x4 slice. The times are simulated.
128 devices in a mesh: expert: 16 (over z_hi, x, core), fsdp: 8 (over z_lo, y).
Axes of the slice: x: 4, y: 4, z: 4 (z_hi: 2, z_lo: 2; z = z_hi * 2 + z_lo), core: 2. Of those that a mesh axis runs over, the one named last changes fastest.
Arguments:
- out_grad: bfloat16 [32768, 7168], P(('expert', 'fsdp')), may hold values from -6 to 6
- expert_ids: int32 [32768, 1], P(('expert', 'fsdp')), may hold values from 0 to 15; in each aligned block of 256 rows (0 to 255, 256 to 511, ...) at most 48 rows name the same one
- stash_codes: bfloat16 [16, 8, 16, 48, 2048], P('expert', 'fsdp'), may hold values from -4 to 4
- stash_scale: int32 [16, 8, 16, 48, 16], P('expert', 'fsdp'), may hold values from -2 to 1
- down_weight: bfloat16 [16, 1024, 7168], P('expert', None, 'fsdp'), may hold values from -0.1875 to 0.1875
Outputs:
- in_grad: bfloat16 [32768, 2048], P(('expert', 'fsdp'))
- weight_grad: bfloat16 [16, 1024, 7168], P('expert', None, 'fsdp')
Inputs may be any that keep to these rules, and one draw needn't show every extreme that they name: `expert_ids`: among the 256 rows of one device, at most 48 name the same expert, and in every draw some device has an expert named by exactly 48 of its rows.
All inputs are finite; a program needn't handle non-finite values.
Results may differ from a plain program's by a relative error of at most 0.017.
Values may be sent and summed in bfloat16 or wider, within the bound.
A program may use at most 192 MiB of HBM per device.

v0:
```python
import jax
import jax.numpy as jnp
from jax import lax
from jax.sharding import PartitionSpec as P

FFW = 1024
BLOCK = 128


def shards(out_grad, expert_ids, stash_codes, stash_scale, down_weight):
    experts = lax.axis_size("expert")
    expert_of = expert_ids[:, 0]
    capacity = stash_codes.shape[3]
    features = out_grad.shape[1]
    onehot = (expert_of[:, None] == jnp.arange(experts, dtype=jnp.int32)[None, :]).astype(jnp.int32)
    slot_of = jnp.sum((jnp.cumsum(onehot, axis=0) - onehot) * onehot, axis=1)
    outgoing = (
        jnp.zeros((experts, capacity, features), out_grad.dtype)
        .at[expert_of, slot_of]
        .set(out_grad)
    )
    arrived = lax.all_to_all(outgoing, "expert", split_axis=0, concat_axis=0, tiled=True)
    grad_rows = arrived.reshape(-1, features)
    slot_count = grad_rows.shape[0]
    blocks_per_row = 2 * FFW // BLOCK
    stash_values = stash_codes[0, 0].reshape(slot_count, blocks_per_row, BLOCK).astype(jnp.float32)
    factor = jnp.exp2(stash_scale[0, 0].reshape(slot_count, blocks_per_row).astype(jnp.float32))
    stash_values = (stash_values * factor[:, :, None]).reshape(slot_count, 2 * FFW)
    gate_value = stash_values[:, :FFW]
    up_value = stash_values[:, FFW:]
    sigmoid_gate = jax.nn.sigmoid(gate_value)
    silu_gate = gate_value * sigmoid_gate
    hidden = (silu_gate * up_value).astype(jnp.bfloat16)
    d_hidden = lax.dot_general(
        grad_rows,
        lax.all_gather(down_weight[0], "fsdp", axis=1, tiled=True),
        (((1,), (1,)), ((), ())),
        preferred_element_type=jnp.float32,
    )
    d_up = d_hidden * silu_gate
    d_gate = d_hidden * up_value * sigmoid_gate * (1.0 + gate_value * (1.0 - sigmoid_gate))
    returned_rows = (
        jnp.concatenate([d_gate, d_up], axis=1)
        .astype(jnp.bfloat16)
        .reshape(experts, capacity, 2 * FFW)
    )
    came_back = lax.all_to_all(returned_rows, "expert", split_axis=0, concat_axis=0, tiled=True)
    in_grad = came_back[expert_of, slot_of]
    weight_term = lax.dot_general(
        hidden, grad_rows, (((0,), (0,)), ((), ())), preferred_element_type=jnp.float32
    )
    summed = lax.psum_scatter(
        weight_term.astype(jnp.bfloat16), "fsdp", scatter_dimension=1, tiled=True
    )
    weight_grad = summed[None]
    return (in_grad, weight_grad)


def solution(mesh):
    placed = (
        P(("expert", "fsdp"), None),
        P(("expert", "fsdp"), None),
        P("expert", "fsdp", None, None, None),
        P("expert", "fsdp", None, None, None),
        P("expert", None, "fsdp"),
    )
    return jax.shard_map(
        shards,
        mesh=mesh,
        in_specs=placed,
        out_specs=(P(("expert", "fsdp"), None), P("expert", None, "fsdp")),
        check_vma=False,
    )
```

profile of v0, /device:TPU:1, one launch (start us, length us, event | category | flops | bytes accessed | tf_op | source)
XLA Modules:
  0.0 533.4 jit_solution(16860895840103120717)
XLA Ops:
  7.2 0.0 all-gather.3.cloned.1.call-start
  7.2 0.7 all-gather.3.cloned.1.call-update
  7.9 0.7 fusion.7
  8.6 0.6 reduce-window.6
  9.2 0.2 slice_reduce_fusion
  9.4 0.8 fusion.6
  10.2 0.7 or_select_fusion
  10.8 5.4 %broadcast_in_dim.4 = bf16[16,48,7168]{2,1,0:T(8,128)(2,1)} broadcast(bf16[]{:T(256)} %constant.6.clone.1), dimensions={} | broadcast | bytes 11010050 | tf_op jit(solution)/shard_map/broadcast_in_dim | solution.py:18
  16.3 96.3 %scatter_fusion = bf16[16,48,7168]{2,1,0:T(8,128)(2,1)} fusion(bf16[16,48,7168]{2,1,0:T(8,128)(2,1)} %broadcast_in_dim.4, s32[256]{0:T(256)S(1)} %bitcast.47, bf16[256,7168]{1,0:T(8,128)(2,1)} %param.5), kind=kCustom, calls=%fused_computation.1 | custom fusion | bytes 11012096 | tf_op jit(solution)/shard_map/scatter | solution.py:20
  112.5 0.0 copy-start.1
  112.5 9.1 %all-to-all-start = ((bf16[16,48,7168]{2,1,0:T(8,128)(2,1)}), bf16[16,48,7168]{2,1,0:T(8,128)(2,1)}, u32[]{:S(2)}, u32[]{:S(2)}) async-start(bf16[16,48,7168]{2,1,0:T(8,128)(2,1)} %scatter_fusion), calls=%async_computation | async-start | bytes 22020096 | tf_op jit(solution)/shard_map/all_to_all | solution.py:22
  121.7 0.2 reduce-scatter.4.cloned.1.call-start
  121.9 0.0 copy-done.1
  121.9 0.2 copy.13
  122.1 0.0 copy-start
  122.1 1.8 mul.36
  123.9 0.1 copy-done
  124.0 6.4 %bitcast_multiply_fusion = f32[768,2048]{1,0:T(8,128)} fusion(f32[96,8,16,128]{3,2,1,0:T(8,128)S(1)} %bitcast.45, bf16[1,1,16,48,2048]{4,3,2,1,0:T(8,128)(2,1)S(1)} %copy-done), kind=kLoop, calls=%fused_computation.5 | loop fusion | flops 3145728 | bytes 15728640 | tf_op jit(solution)/shard_map/mul | solution.py:28
  130.4 164.7 %all-to-all-done = bf16[16,48,7168]{2,1,0:T(8,128)(2,1)} async-done(((bf16[16,48,7168]{2,1,0:T(8,128)(2,1)}), bf16[16,48,7168]{2,1,0:T(8,128)(2,1)}, u32[]{:S(2)}, u32[]{:S(2)}) %all-to-all-start) | async-done | bytes 11010080 | tf_op jit(solution)/shard_map/all_to_all | solution.py:22
  295.1 19.6 %convolution_convert_fusion = bf16[1024,7168]{1,0:T(8,128)(2,1)} fusion(bf16[768,7168]{1,0:T(8,128)(2,1)} %bitcast.5, f32[768,2048]{1,0:T(8,128)} %bitcast_multiply_fusion), kind=kOutput, calls=%fused_computation.4 | convolution fusion | flops 11286347776 | bytes 31981568 | tf_op jit(solution)/shard_map/dot_general | solution.py:49
  314.7 19.9 %copy.14 = bf16[1024,7168]{0,1:T(8,128)(2,1)} copy(bf16[1024,7168]{1,0:T(8,128)(2,1)} %convolution_convert_fusion) | data formatting | bytes 29360128
  334.6 0.0 reduce-scatter.4.cloned.1.call-update
  334.6 0.0 all-gather.3.cloned.1.call-done
  334.7 22.0 %multiply_convert_fusion.2 = (bf16[768,1024]{1,0:T(8,128)(2,1)S(1)}, bf16[768,1024]{1,0:T(8,128)(2,1)S(1)}) fusion(f32[768,2048]{1,0:T(8,128)} %bitcast_multiply_fusion, bf16[768,7168]{1,0:T(8,128)(2,1)} %bitcast.5, bf16[1,1024,7168]{2,1,0:T(8,128)(2,1)} %all-gather.3.cloned.1.call-done), kind=kOutput, calls=%fused_computation.9 | convolution fusion | flops 11284512768 | bytes 35127296 | tf_op jit(solution)/shard_map/dot_general | solution.py:34
  356.6 0.3 pad_maximum_fusion
  356.9 160.5 %all_to_all.10 = bf16[16,48,2048]{2,1,0:T(8,128)(2,1)S(1)} all-to-all(bf16[16,48,2048]{2,1,0:T(8,128)(2,1)S(1)} %pad_maximum_fusion), channel_id=1, replica_groups=mesh['expert'=16,'fsdp'=8] {'expert'}, dimensions={0} | all-to-all | bytes 6291456 | tf_op jit(solution)/shard_map/all_to_all | solution.py:47
  517.5 5.3 gather_fusion
  522.8 0.0 reduce-scatter.4.cloned.1.call-done
  522.8 3.8 copy.15
  (3 shorter events, 0.1 us)
Async XLA Ops:
  7.2 327.5 %all-gather.3.cloned.1.call-start = ((), (), s32[]{:S(2)}) async-start(), calls=%async_computation.3 | async-start | bytes 16515072 | tf_op jit(solution)/shard_map/all_gather | solution.py:36
  112.5 9.4 %copy-start.1 = (s32[1,1,16,48,16]{3,4,2,1,0:T(8,128)S(1)}, s32[1,1,16,48,16]{3,4,2,1,0:T(8,128)}, u32[]{:S(2)}) copy-start(s32[1,1,16,48,16]{3,4,2,1,0:T(8,128)} %param.8) | copy-start | bytes 147460
  112.5 182.5 %all-to-all-start = ((bf16[16,48,7168]{2,1,0:T(8,128)(2,1)}), bf16[16,48,7168]{2,1,0:T(8,128)(2,1)}, u32[]{:S(2)}, u32[]{:S(2)}) async-start(bf16[16,48,7168]{2,1,0:T(8,128)(2,1)} %scatter_fusion), calls=%async_computation | async-start | bytes 22020096 | tf_op jit(solution)/shard_map/all_to_all | solution.py:22
  121.7 401.1 %reduce-scatter.4.cloned.1.call-start = ((), (), s32[]{:S(2)}) async-start(), calls=%async_computation.4 | async-start | bytes 16515072
  122.1 1.9 copy-start
Sparse Core Ops, SparseCore 0:
  9.7 198.4 all-gather.2
  334.7 174.3 reduce-scatter.3
where the time goes:
time: 535 us; the launch traced here: 533 us
  waiting for transfers between devices  165 us (31%)
  blocking collectives  161 us (30%)
  local copies, waits for them, and re-layouts  133 us (25%)
  matrix products  41.6 us (8%)
  between operations  14.1 us (3%)
  other arithmetic  9.43 us (2%)
  starting transfers between devices  9.38 us (2%)
    all_to_all x1, waiting for transfers between devices, shards(): lax.all_to_all(outgoing, 'expert', split_axis=0, concat_axis=0, tiled=True)  165 us
    all_to_all x1, blocking collectives, shards(): lax.all_to_all(returned_rows, 'expert', split_axis=0, concat_axis=0, tile...  161 us
    scatter x1, local copies, waits for them, and re-layouts, shards(): outgoing = jnp.zeros((experts, capacity, features), out_grad.dtype).at[ex...  96.3 us
    unnamed x6, local copies, waits for them, and re-layouts  23.8 us
    dot_general x1, matrix products, shards(): lax.dot_general(grad_rows, lax.all_gather(down_weight[0], 'fsdp', axis=1,...  22 us
    dot_general x1, matrix products, shards(): lax.dot_general(hidden, grad_rows, (((0,), (0,)), ((), ())), preferred_el...  19.6 us
  transfers between devices with their start and end apart: 3, of which 1 were waited for; matrix products, arithmetic and copies ran while one was open for 34% of the time, Pallas kernels for 0%

commit v1 on v0

v1 whole, which is shorter than its diff:
```python
import jax
import jax.numpy as jnp
from jax import lax
from jax.experimental import pallas as pl
from jax.experimental.pallas import tpu as pltpu
from jax.sharding import PartitionSpec as P

FFW = 1024
BLOCK = 128
CAP = 48
ROWS = 256
FEAT = 896
HALF = 8 * CAP
SLOTS = 2 * HALF
OUTS = 3
PARTS = 4
PCOLS = 2 * FFW // PARTS
MESH = pl.DeviceIdType.MESH
BF = jnp.bfloat16
F32 = jnp.float32


def kernel(
    grad, ids, stash, scale, weight,
    in_grad, weight_grad, parts,
    raw, out, rows, wts, hidden, coef, dh, dh_out, dh_in, back, ret, pick, pick_t, keys, fin_out, fin_in,
    raw_s, raw_r, key_s, key_r, w_s, w_r, x_s, x_r, hid_s, hid_r, dh_s, dh_r, part_s, part_r, ret_s, ret_r, fin_s, fin_r,
    own_sem, stash_sem, self_sem, load_sem,
):
    e = lax.axis_index("expert")
    f = lax.axis_index("fsdp")
    zh, x, c = e // 8, (e // 2) % 4, e % 2
    zl, y = f // 4, f % 4

    def z_peer(d):
        h = 1 - zh if d & 2 else zh
        l = 1 - zl if d & 1 else zl
        return (h * 8 + x * 2 + c, l * 4 + y)

    def xc(k, sign):
        dx, dc = k // 2, k % 2
        return lax.rem(x + (4 + sign * dx), 4), (1 - c if dc else c)

    def x_peer(k, sign):
        px, pc = xc(k, sign)
        return (zh * 8 + px * 2 + pc, f)

    def y_peer(j):
        return (e, zl * 4 + lax.rem(y + 4 + j, 4))

    def remote(src, dst, s, r, device):
        return pltpu.make_async_remote_copy(
            src_ref=src, dst_ref=dst, send_sem=s, recv_sem=r, device_id=device, device_id_type=MESH
        )

    barrier = pltpu.get_barrier_semaphore()
    peers = [z_peer(d) for d in (1, 2, 3)] + [x_peer(k, 1) for k in range(1, 8)] + [y_peer(j) for j in (1, 2, 3)]
    for peer in peers:
        pl.semaphore_signal(barrier, inc=1, device_id=peer, device_id_type=MESH)

    def columns(half, step):
        quarter = lax.rem(y + step, 4)
        return pl.ds(pl.multiple_of((half * 4 + quarter) * FEAT, 128), FEAT)

    stash_copies = []
    for s in range(16):
        sx, sc = xc(s % 8, -1)
        g = (1 - zh if s // 8 else zh) * 8 + sx * 2 + sc
        stash_copies.append(
            pltpu.make_async_copy(stash.at[0, 0, g], back.at[s // 8, pl.ds((s % 8) * CAP, CAP)], stash_sem.at[s])
        )
    own_weight = pltpu.make_async_copy(weight.at[0], wts.at[0], own_sem.at[4])
    own_rows = [
        pltpu.make_async_copy(grad.at[:, columns(zl, i + 1)], raw.at[0, i], own_sem.at[i]) for i in range(4)
    ]
    own_weight.start()
    for copy in stash_copies + own_rows:
        copy.start()

    expert_of = ids[...]
    same = lax.broadcasted_iota(jnp.int32, (16, ROWS), 0) == expert_of
    chosen = jnp.where(same, 1.0, 0.0)
    earlier = jnp.where(
        lax.broadcasted_iota(jnp.int32, (ROWS, ROWS), 0) < lax.broadcasted_iota(jnp.int32, (ROWS, ROWS), 1), 1.0, 0.0
    )
    count = jnp.dot(chosen.astype(BF), earlier.astype(BF), preferred_element_type=F32)
    slot = jnp.sum(chosen * count, axis=0, keepdims=True)
    key = expert_of * CAP + slot.astype(jnp.int32)
    keys[0] = jnp.broadcast_to(key, (8, ROWS))

    pl.semaphore_wait(barrier, len(peers))

    raw_copies = {}
    for i in range(4):
        for d in (1, 3):
            raw_copies[d, i] = remote(
                grad.at[:, columns(1 - zl, i)], raw.at[d, i], raw_s.at[d, i], raw_r.at[d, i], z_peer(d)
            )
        raw_copies[2, i] = remote(
            grad.at[:, columns(zl, i + 1)], raw.at[2, i], raw_s.at[2, i], raw_r.at[2, i], z_peer(2)
        )
    key_copies = [remote(keys.at[0], keys.at[d], key_s.at[d], key_r.at[d], z_peer(d)) for d in (1, 2, 3)]
    weight_copies = [remote(weight.at[0], wts.at[j], w_s.at[j], w_r.at[j], y_peer(-j)) for j in (1, 2, 3)]
    for copy in key_copies:
        copy.start()
    for i in range(4):
        raw_copies[1, i].start()
        raw_copies[3, i].start()
    for copy in weight_copies:
        copy.start()

    place = lax.broadcasted_iota(jnp.int32, (CAP, ROWS), 0)

    def make_pick(d):
        key_of = keys[d, 0:1, :]
        for k in range(8):
            px, pc = xc(k, 1)
            base = (zh * 8 + px * 2 + pc) * CAP
            pick[d, k * CAP : (k + 1) * CAP, :] = jnp.where(key_of - base == place, 1.0, 0.0).astype(BF)

    for copy in key_copies:
        copy.wait_recv()
    for d in range(4):
        make_pick(d)

    x_copies = {}

    def dispatch(s):
        group, i = s // 4, s % 4
        slot_of = s % OUTS
        if s >= OUTS:
            for copy in x_copies[s - OUTS]:
                copy.wait_send()
        for zr in range(2):
            d = 2 * zr + (1 - group)
            if d == 0:
                own_rows[i].wait()
            else:
                raw_copies[d, i].wait_recv()

            def tile(t, _, zr=zr, d=d):
                at = pl.ds(pl.multiple_of(t * 192, 192), 192)
                put = jnp.dot(pick[d, at, :], raw[d, i], preferred_element_type=F32)
                out[slot_of, zr, at, :] = put.astype(BF)
                return 0

            lax.fori_loop(0, 2, tile, 0)
            rows[group, i, zr, 0:CAP, :] = out[slot_of, zr, 0:CAP, :]
        x_copies[s] = []
        for k in range(1, 8):
            block = pl.ds(k * CAP, CAP)
            copy = remote(
                out.at[slot_of, :, block, :], rows.at[group, i, :, block, :], x_s.at[s, k], x_r.at[s, k], x_peer(k, 1)
            )
            copy.start()
            x_copies[s].append(copy)

    dispatch(0)
    dispatch(1)
    raw_copies[2, 0].start()
    raw_copies[2, 1].start()

    for copy in stash_copies:
        copy.wait()

    def gate_tile(s, _):
        zr, k = s // 8, s % 8
        dx, dc = k // 2, k % 2
        sx = lax.rem(x + 4 - dx, 4)
        sc = c + dc - 2 * c * dc
        sz = zh + zr - 2 * zh * zr
        factor = jnp.exp2(scale[sz * 8 + sx * 2 + sc].astype(F32))
        at = pl.ds(pl.multiple_of(k * CAP, CAP), CAP)
        flat = pl.ds(pl.multiple_of(s * CAP, CAP), CAP)
        for b in range(FFW // BLOCK):
            low, high = slice(b * BLOCK, (b + 1) * BLOCK), slice(FFW + b * BLOCK, FFW + (b + 1) * BLOCK)
            gate = back[zr, at, low].astype(F32) * factor[:, b : b + 1]
            up = back[zr, at, high].astype(F32) * factor[:, 8 + b : 9 + b]
            sig = 1.0 / (1.0 + jnp.exp(-gate))
            silu = gate * sig
            dh_out[flat, low] = (silu * up).astype(BF)
            coef[flat, low] = (up * sig * (1.0 + gate * (1.0 - sig))).astype(BF)
            coef[flat, high] = silu.astype(BF)
        return 0

    lax.fori_loop(0, 16, gate_tile, 0)

    def turn(b, _):
        at = pl.ds(pl.multiple_of(b * BLOCK, BLOCK), BLOCK)
        hidden[0, at, :] = dh_out[:, at].T
        return 0

    lax.fori_loop(0, FFW // BLOCK, turn, 0)
    for n, d in enumerate((0, 2)):
        pick_t[n] = pick[d].astype(F32).T.astype(BF)
    hidden_copy = remote(hidden.at[0], hidden.at[1], hid_s.at[0], hid_r.at[0], z_peer(1))
    hidden_copy.start()

    def d_hidden(group, i, w):
        def tile(n, _):
            at = pl.ds(pl.multiple_of(n * 256, 256), 256)
            term = lax.dot_general(
                rows[group, i].reshape(SLOTS, FEAT), wts[w, at, :], (((1,), (1,)), ((), ())), preferred_element_type=F32
            )
            if i == 0:
                dh[:, at] = term
            else:
                dh[:, at] += term
            return 0

        lax.fori_loop(0, FFW // 256, tile, 0)

    def partial(i, earlier_step, into):
        def tile(m, _):
            at = pl.ds(pl.multiple_of(m * 256, 256), 256)
            term = jnp.dot(hidden[0, at, :], rows[1, i].reshape(SLOTS, FEAT), preferred_element_type=F32)
            term += jnp.dot(hidden[1, at, :], rows[0, earlier_step].reshape(SLOTS, FEAT), preferred_element_type=F32)
            wts[into, at, :] = term.astype(BF)
            return 0

        lax.fori_loop(0, FFW // 256, tile, 0)

    part_copies = []
    dh_copy = remote(dh_out, dh_in, dh_s.at[0], dh_r.at[0], z_peer(1))
    for s in range(8):
        group, i = s // 4, s % 4
        for copy in x_copies[s]:
            copy.wait_recv()
        if group == 0:
            if i == 0:
                own_weight.wait()
            else:
                weight_copies[i - 1].wait_recv()
            d_hidden(0, i, i)
            if i == 3:
                dh_out[...] = dh[...].astype(BF)
                dh_copy.start()
        else:
            w = (1 + i) % 4
            d_hidden(1, i, w)
            if i == 0:
                hidden_copy.wait_recv()
            if i < 3:
                partial(i, w, w)
                copy = remote(wts.at[w], parts.at[i], part_s.at[i], part_r.at[i], y_peer(1 + i))
                copy.start()
                part_copies.append(copy)
        if s + 2 < 8:
            dispatch(s + 2)
        if s in (0, 1):
            raw_copies[2, 2 + s].start()

    dh_copy.wait_recv()
    ret_copies, self_copies, fin_copies = {}, [], []
    for p in range(PARTS):
        cols = pl.ds(p * PCOLS, PCOLS)
        dh_cols = pl.ds((p % 2) * PCOLS, PCOLS)

        def back_tile(s, _, cols=cols, dh_cols=dh_cols):
            at = pl.ds(pl.multiple_of((s % 8) * CAP, CAP), CAP)
            flat = pl.ds(pl.multiple_of(s * CAP, CAP), CAP)
            total = dh[flat, dh_cols] + dh_in[flat, dh_cols].astype(F32)
            back[s // 8, at, cols] = (total * coef[flat, cols].astype(F32)).astype(BF)
            return 0

        lax.fori_loop(0, 16, back_tile, 0)
        here = pltpu.make_async_copy(back.at[:, pl.ds(0, CAP), cols], ret.at[:, pl.ds(0, CAP), cols], self_sem.at[p])
        here.start()
        self_copies.append(here)
        ret_copies[p] = []
        for k in range(1, 8):
            block = pl.ds(k * CAP, CAP)
            copy = remote(
                back.at[:, block, cols], ret.at[:, block, cols], ret_s.at[p, k], ret_r.at[p, k], x_peer(k, -1)
            )
            copy.start()
            ret_copies[p].append(copy)

    partial(3, 0, 0)

    for p in range(PARTS):
        cols = pl.ds(p * PCOLS, PCOLS)
        self_copies[p].wait()
        for copy in ret_copies[p]:
            copy.wait_recv()
        fin_out[:, cols] = jnp.dot(pick_t[1], ret[1, :, cols], preferred_element_type=F32).astype(BF)
        copy = remote(fin_out.at[:, cols], fin_in.at[:, cols], fin_s.at[p], fin_r.at[p], z_peer(2))
        copy.start()
        fin_copies.append(copy)
        in_grad[:, cols] = jnp.dot(pick_t[0], ret[0, :, cols], preferred_element_type=F32).astype(BF)

    loads = []
    for i in range(3):
        part_copies[i].wait_recv()
        part_copies[i].wait_send()
        load = pltpu.make_async_copy(parts.at[i], wts.at[1 + i], load_sem.at[i])
        load.start()
        loads.append(load)
    for load in loads:
        load.wait()

    def sum_tile(t, _):
        at = pl.ds(pl.multiple_of(t * 64, 64), 64)
        total = wts[0, at, :].astype(F32)
        for i in range(1, 4):
            total += wts[i, at, :].astype(F32)
        weight_grad[0, at, :] = total.astype(BF)
        return 0

    lax.fori_loop(0, FFW // 64, sum_tile, 0)

    for p in range(PARTS):
        cols = pl.ds(p * PCOLS, PCOLS)
        fin_copies[p].wait_recv()
        in_grad[:, cols] = in_grad[:, cols] + fin_in[:, cols]

    sent = list(raw_copies.values()) + key_copies + weight_copies + [hidden_copy, dh_copy] + fin_copies
    for s in range(8 - OUTS, 8):
        sent += x_copies[s]
    for p in range(PARTS):
        sent += ret_copies[p]
    for copy in sent:
        copy.wait_send()


def shards(out_grad, expert_ids, stash_codes, stash_scale, down_weight):
    dma = pltpu.SemaphoreType.DMA
    hbm = pl.BlockSpec(memory_space=pl.ANY)
    vmem = pl.BlockSpec(memory_space=pltpu.VMEM)
    scratch = [
        pltpu.VMEM((4, 4, ROWS, FEAT), BF),
        pltpu.VMEM((OUTS, 2, HALF, FEAT), BF),
        pltpu.VMEM((2, 4, 2, HALF, FEAT), BF),
        pltpu.VMEM((4, FFW, FEAT), BF),
        pltpu.VMEM((2, FFW, SLOTS), BF),
        pltpu.VMEM((SLOTS, 2 * FFW), BF),
        pltpu.VMEM((SLOTS, FFW), F32),
        pltpu.VMEM((SLOTS, FFW), BF),
        pltpu.VMEM((SLOTS, FFW), BF),
        pltpu.VMEM((2, HALF, 2 * FFW), BF),
        pltpu.VMEM((2, HALF, 2 * FFW), BF),
        pltpu.VMEM((4, HALF, ROWS), BF),
        pltpu.VMEM((2, ROWS, HALF), BF),
        pltpu.VMEM((4, 8, ROWS), jnp.int32),
        pltpu.VMEM((ROWS, 2 * FFW), BF),
        pltpu.VMEM((ROWS, 2 * FFW), BF),
    ]
    pairs = [(4, 4), (4,), (4,), (8, 8), (1,), (1,), (3,), (PARTS, 8), (PARTS,)]
    for shape in pairs:
        scratch += [dma(shape), dma(shape)]
    scratch += [dma((5,)), dma((16,)), dma((PARTS,)), dma((3,))]
    in_grad, weight_grad, _ = pl.pallas_call(
        kernel,
        out_shape=(
            jax.ShapeDtypeStruct((ROWS, 2 * FFW), BF),
            jax.ShapeDtypeStruct((1, FFW, FEAT), BF),
            jax.ShapeDtypeStruct((3, FFW, FEAT), BF),
        ),
        in_specs=[hbm, vmem, hbm, vmem, hbm],
        out_specs=(vmem, vmem, hbm),
        scratch_shapes=scratch,
        compiler_params=pltpu.CompilerParams(
            collective_id=0, has_side_effects=True, vmem_limit_bytes=60 * 2**20
        ),
        name="expert_backward",
    )(out_grad, expert_ids.reshape(1, ROWS), stash_codes, stash_scale[0, 0], down_weight)
    return in_grad, weight_grad


def solution(mesh):
    placed = (
        P(("expert", "fsdp"), None),
        P(("expert", "fsdp"), None),
        P("expert", "fsdp", None, None, None),
        P("expert", "fsdp", None, None, None),
        P("expert", None, "fsdp"),
    )
    return jax.shard_map(
        shards,
        mesh=mesh,
        in_specs=placed,
        out_specs=(P(("expert", "fsdp"), None), P("expert", None, "fsdp")),
        check_vma=False,
    )
```

time: 535 us -> 223 us (0.42)
  Pallas kernels: 0 us -> 217 us
  waiting for transfers between devices: 165 us -> 0 us
  blocking collectives: 161 us -> 0 us
  local copies, waits for them, and re-layouts: 133 us -> 5.5 us
  matrix products: 41.6 us -> 0 us
  between operations: 14.1 us -> 0.65 us
  other arithmetic: 9.43 us -> 0 us
  starting transfers between devices: 9.38 us -> 0 us
    pallas_call x0 -> x1, Pallas kernels: none -> 217 us  [shards(): pl.pallas_call(kernel, out_shape=(jax.ShapeDtypeStruct((ROWS, 2 * FFW), B...]
    all_to_all x1 -> x0, waiting for transfers between devices: 165 us -> none  [shards(): lax.all_to_all(outgoing, 'expert', split_axis=0, concat_axis=0, tiled=True)]
    all_to_all x1 -> x0, blocking collectives: 161 us -> none  [shards(): lax.all_to_all(returned_rows, 'expert', split_axis=0, concat_axis=0, tile...]
    scatter x1 -> x0, local copies, waits for them, and re-layouts: 96.3 us -> none  [shards(): outgoing = jnp.zeros((experts, capacity, features), out_grad.dtype).at[ex...]
    dot_general x2 -> x0, matrix products: 41.6 us -> none  [the longest x1 22 us: shards(): lax.dot_general(grad_rows, lax.all_gather(down_weight[0], 'fsdp', axis=1,...]
    unnamed x6 -> x5, local copies, waits for them, and re-layouts: 23.8 us -> 5.5 us
    all_to_all x1 -> x0, starting transfers between devices: 9.12 us -> none  [shards(): lax.all_to_all(outgoing, 'expert', split_axis=0, concat_axis=0, tiled=True)]
    mul x1 -> x0, other arithmetic: 6.37 us -> none  [shards(): stash_values * factor[:, :, None]]
  transfers between devices with their start and end apart: 3 -> 0, of which waited for: 1 -> 0; matrix products, arithmetic and copies ran while one was open for 34% -> 0% of each run, Pallas kernels for 0% -> 0%
where the time goes in v1:
time: 223 us
  Pallas kernels  217 us (97%)
  local copies, waits for them, and re-layouts  5.5 us (2%)
    pallas_call x1, Pallas kernels, shards(): pl.pallas_call(kernel, out_shape=(jax.ShapeDtypeStruct((ROWS, 2 * FFW), B...  217 us
    unnamed x5, local copies, waits for them, and re-layouts  5.5 us

profile of v1, /device:TPU:1, one launch (start us, length us, event | category | flops | bytes accessed | tf_op | source)
XLA Modules:
  0.0 223.1 jit_solution(331353687778439025)
XLA Ops:
  0.6 1.8 copy.7
  2.5 216.9 %expert_backward.1 = (bf16[256,2048]{1,0:T(8,128)(2,1)}, bf16[1,1024,896]{2,1,0:T(8,128)(2,1)}, bf16[3,1024,896]{2,1,0:T(8,128)(2,1)}) custom-call(bf16[256,7168]{1,0:T(8,128)(2,1)} %grad.1, s32[1,256]{1,0:T(1,128)} %bitcast.3, bf16[1,1,16,48,2048]{4,3,2,1,0:T(8,128)(2,1)} %stash.1, s32[16,48,16]{2,1,0:T(8,128)} %bitcast.2, bf16[1,1024,896]{2,1,0:T(8,128)(2,1)} %weight.1), custom_call_target="tpu_custom_call" | custom-call | tf_op jit(solution)/shard_map/expert_backward/pallas_call | solution.py:352
  219.4 0.0 copy-start
  219.4 2.4 %copy.10 = bf16[256,2048]{1,0:T(8,128)(2,1)} copy(bf16[256,2048]{1,0:T(8,128)(2,1)} %get-tuple-element.8) | data formatting | bytes 2097152
  221.8 0.0 copy-done
  221.8 1.2 copy.11
Async XLA Ops:
  219.4 2.5 %copy-start = (bf16[1,1024,896]{2,1,0:T(8,128)(2,1)S(1)}, bf16[1,1024,896]{2,1,0:T(8,128)(2,1)}, u32[]{:S(2)}) copy-start(bf16[1,1024,896]{2,1,0:T(8,128)(2,1)} %get-tuple-element.9) | copy-start | bytes 5505028

commit v2 on v0

v2 whole, which is shorter than its diff:
```python
import jax
import jax.numpy as jnp
from jax import lax
from jax.experimental import pallas as pl
from jax.experimental.pallas import tpu as pltpu
from jax.sharding import PartitionSpec as P

FFW = 1024
BLOCK = 128
CAP = 48
ROWS = 256
FEAT = 896
HALF = 8 * CAP
SLOTS = 2 * HALF
OUTS = 8
ORDER = (2, 1, 3, 0)
PARTS = 4
PCOLS = 2 * FFW // PARTS
MESH = pl.DeviceIdType.MESH
BF = jnp.bfloat16
F32 = jnp.float32


def kernel(
    grad, ids, stash, scale_in, weight,
    own_grad, far_grad, parts,
    raw, out, rows, wts, hidden, coef, dh, dh_out, dh_in, back, ret, pick, pick_t, keys, fin, scale,
    raw_s, raw_r, key_s, key_r, w_s, w_r, x_s, x_r, hid_s, hid_r, dh_s, dh_r, part_s, part_r, ret_s, ret_r, fin_s, fin_r,
    own_sem, stash_sem, self_sem, store_sem,
):
    e = lax.axis_index("expert")
    f = lax.axis_index("fsdp")
    zh, x, c = e // 8, (e // 2) % 4, e % 2
    zl, y = f // 4, f % 4

    def z_peer(d):
        h = 1 - zh if d & 2 else zh
        l = 1 - zl if d & 1 else zl
        return (h * 8 + x * 2 + c, l * 4 + y)

    def xc(k, sign):
        dx, dc = k // 2, k % 2
        return lax.rem(x + (4 + sign * dx), 4), (1 - c if dc else c)

    def x_peer(k, sign):
        px, pc = xc(k, sign)
        return (zh * 8 + px * 2 + pc, f)

    def y_peer(j):
        return (e, zl * 4 + lax.rem(y + 4 + j, 4))

    def remote(src, dst, s, r, device):
        return pltpu.make_async_remote_copy(
            src_ref=src, dst_ref=dst, send_sem=s, recv_sem=r, device_id=device, device_id_type=MESH
        )

    barrier = pltpu.get_barrier_semaphore()
    peers = [z_peer(d) for d in (1, 2, 3)] + [x_peer(k, 1) for k in range(1, 8)] + [y_peer(j) for j in (1, 2, 3)]
    for peer in peers:
        pl.semaphore_signal(barrier, inc=1, device_id=peer, device_id_type=MESH)

    def columns(half, j):
        quarter = lax.rem(y + j, 4)
        return pl.ds(pl.multiple_of((half * 4 + quarter) * FEAT, 128), FEAT)

    own_rows = {
        j: pltpu.make_async_copy(grad.at[:, columns(zl, j)], raw.at[0, j], own_sem.at[j]) for j in ORDER
    }
    stash_copies = [pltpu.make_async_copy(scale_in.at[0, 0], scale, own_sem.at[5])]
    for s in range(16):
        sx, sc = xc(s % 8, -1)
        g = (1 - zh if s // 8 else zh) * 8 + sx * 2 + sc
        stash_copies.append(
            pltpu.make_async_copy(stash.at[0, 0, g], back.at[s // 8, pl.ds((s % 8) * CAP, CAP)], stash_sem.at[s])
        )
    own_weight = pltpu.make_async_copy(weight.at[0], wts.at[0], own_sem.at[4])
    for j in ORDER:
        own_rows[j].start()
    for copy in stash_copies:
        copy.start()
    own_weight.start()

    expert_of = ids[...]
    same = lax.broadcasted_iota(jnp.int32, (16, ROWS), 0) == expert_of
    chosen = jnp.where(same, 1.0, 0.0)
    earlier = jnp.where(
        lax.broadcasted_iota(jnp.int32, (ROWS, ROWS), 0) < lax.broadcasted_iota(jnp.int32, (ROWS, ROWS), 1), 1.0, 0.0
    )
    count = jnp.dot(chosen.astype(BF), earlier.astype(BF), preferred_element_type=F32)
    slot = jnp.sum(chosen * count, axis=0, keepdims=True)
    key = expert_of * CAP + slot.astype(jnp.int32)
    keys[0] = jnp.broadcast_to(key, (8, ROWS))

    place = lax.broadcasted_iota(jnp.int32, (CAP, ROWS), 0)

    def make_pick(d):
        key_of = keys[d, 0:1, :]
        for k in range(8):
            px, pc = xc(k, 1)
            base = (zh * 8 + px * 2 + pc) * CAP
            pick[d, k * CAP : (k + 1) * CAP, :] = jnp.where(key_of - base == place, 1.0, 0.0).astype(BF)

    make_pick(0)
    pl.semaphore_wait(barrier, len(peers))

    raw_copies = {
        (d, j): remote(
            grad.at[:, columns(1 - zl if d & 1 else zl, j)], raw.at[d, j], raw_s.at[d, j], raw_r.at[d, j], z_peer(d)
        )
        for d in (1, 2, 3)
        for j in ORDER
    }
    key_copies = [remote(keys.at[0], keys.at[d], key_s.at[d], key_r.at[d], z_peer(d)) for d in (1, 2, 3)]
    weight_copies = {j: remote(weight.at[0], wts.at[j], w_s.at[j], w_r.at[j], y_peer(-j)) for j in (1, 2, 3)}
    hidden_copy = remote(hidden.at[0], hidden.at[1], hid_s.at[0], hid_r.at[0], z_peer(1))
    dh_copies = [remote(dh_out.at[zr], dh_in.at[zr], dh_s.at[zr], dh_r.at[zr], z_peer(1)) for zr in range(2)]
    part_copies = {
        j: remote(wts.at[j], parts.at[j - 1], part_s.at[j - 1], part_r.at[j - 1], y_peer(j)) for j in (1, 2, 3)
    }

    x_copies = {}
    order = []

    def dispatch(d, j):
        unit = len(order)
        into = unit % OUTS
        if unit >= OUTS:
            for copy in x_copies[order[unit - OUTS]]:
                copy.wait_send()
        order.append((d, j))
        if d == 0:
            own_rows[j].wait()
        else:
            raw_copies[d, j].wait_recv()

        def tile(t, _):
            at = pl.ds(pl.multiple_of(t * 192, 192), 192)
            out[into, at, :] = jnp.dot(pick[d, at, :], raw[d, j], preferred_element_type=F32).astype(BF)
            return 0

        lax.fori_loop(0, 2, tile, 0)
        rows[d, j, 0:CAP, :] = out[into, 0:CAP, :]
        x_copies[d, j] = []
        for k in range(1, 8):
            block = pl.ds(k * CAP, CAP)
            copy = remote(
                out.at[into, block, :], rows.at[d, j, block, :], x_s.at[unit, k], x_r.at[unit, k], x_peer(k, 1)
            )
            copy.start()
            x_copies[d, j].append(copy)

    def gate_tile(s, _):
        zr, k = s // 8, s % 8
        dx, dc = k // 2, k % 2
        sx = lax.rem(x + 4 - dx, 4)
        sc = c + dc - 2 * c * dc
        sz = zh + zr - 2 * zh * zr
        factor = jnp.exp2(scale[sz * 8 + sx * 2 + sc].astype(F32)).T
        at = pl.ds(pl.multiple_of(k * CAP, CAP), CAP)
        for b in range(FFW // BLOCK):
            low, high = slice(b * BLOCK, (b + 1) * BLOCK), slice(FFW + b * BLOCK, FFW + (b + 1) * BLOCK)
            gate = back[zr, at, low].astype(F32) * factor[:, b : b + 1]
            up = back[zr, at, high].astype(F32) * factor[:, 8 + b : 9 + b]
            sig = 1.0 / (1.0 + jnp.exp(-gate))
            silu = gate * sig
            dh_out[zr, at, low] = (silu * up).astype(BF)
            coef[zr, at, low] = (up * sig * (1.0 + gate * (1.0 - sig))).astype(BF)
            coef[zr, at, high] = silu.astype(BF)
        return 0

    def turn(b, _):
        at = pl.ds(pl.multiple_of(b * BLOCK, BLOCK), BLOCK)
        for zr in range(2):
            hidden[0, at, zr * HALF : (zr + 1) * HALF] = dh_out[zr, :, at].T
        return 0

    def d_hidden(d, j):
        for copy in x_copies[d, j]:
            copy.wait_recv()

        def tile(n, _):
            at = pl.ds(pl.multiple_of(n * 256, 256), 256)
            term = lax.dot_general(
                rows[d, j], wts[j, at, :], (((1,), (1,)), ((), ())), preferred_element_type=F32
            )
            if j == ORDER[0]:
                dh[d, :, at] = term
            else:
                dh[d, :, at] += term
            return 0

        lax.fori_loop(0, FFW // 256, tile, 0)

    def partial(j):
        def tile(m, _):
            at = pl.ds(pl.multiple_of(m * 256, 256), 256)
            term = jnp.dot(hidden[0, at, 0:HALF], rows[0, j], preferred_element_type=F32)
            term += jnp.dot(hidden[0, at, HALF:SLOTS], rows[2, j], preferred_element_type=F32)
            term += jnp.dot(hidden[1, at, 0:HALF], rows[1, j], preferred_element_type=F32)
            term += jnp.dot(hidden[1, at, HALF:SLOTS], rows[3, j], preferred_element_type=F32)
            wts[j, at, :] = term.astype(BF)
            return 0

        lax.fori_loop(0, FFW // 256, tile, 0)
        if j:
            part_copies[j].start()

    def exchange(zr):
        dh_out[zr] = dh[1 + 2 * zr].astype(BF)
        dh_copies[zr].start()

    ret_copies, self_copies, fin_copies, store_copies = {}, {}, [], []

    def send_back(zr):
        dh_copies[zr].wait_recv()
        for p in range(PARTS):
            cols = pl.ds(p * PCOLS, PCOLS)
            dh_cols = pl.ds((p * PCOLS) % FFW, PCOLS)

            def back_tile(k, _, cols=cols, dh_cols=dh_cols):
                at = pl.ds(pl.multiple_of(k * CAP, CAP), CAP)
                total = dh[2 * zr, at, dh_cols] + dh_in[zr, at, dh_cols].astype(F32)
                back[zr, at, cols] = (total * coef[zr, at, cols].astype(F32)).astype(BF)
                return 0

            lax.fori_loop(0, 8, back_tile, 0)
            here = pltpu.make_async_copy(
                back.at[zr, pl.ds(0, CAP), cols], ret.at[zr, pl.ds(0, CAP), cols], self_sem.at[zr, p]
            )
            here.start()
            self_copies[zr, p] = here
            ret_copies[zr, p] = []
            for k in range(1, 8):
                block = pl.ds(k * CAP, CAP)
                copy = remote(
                    back.at[zr, block, cols], ret.at[zr, block, cols],
                    ret_s.at[zr, p, k], ret_r.at[zr, p, k], x_peer(k, -1),
                )
                copy.start()
                ret_copies[zr, p].append(copy)

    def collect(zr, p):
        cols = pl.ds(p * PCOLS, PCOLS)
        self_copies[zr, p].wait()
        for copy in ret_copies[zr, p]:
            copy.wait_recv()
        fin[zr, :, cols] = jnp.dot(pick_t[zr], ret[zr, :, cols], preferred_element_type=F32).astype(BF)
        if zr:
            copy = remote(fin.at[1, :, cols], far_grad.at[:, cols], fin_s.at[p], fin_r.at[p], z_peer(2))
            fin_copies.append(copy)
        else:
            copy = pltpu.make_async_copy(fin.at[0, :, cols], own_grad.at[:, cols], store_sem.at[p])
            store_copies.append(copy)
        copy.start()

    a, b, g, o = ORDER
    for copy in key_copies:
        copy.start()
    for d in (1, 3, 2):
        raw_copies[d, a].start()
    weight_copies[a].start()
    dispatch(0, a)
    dispatch(0, b)
    for copy in key_copies:
        copy.wait_recv()
    for d in (1, 3, 2):
        make_pick(d)
    for copy in stash_copies:
        copy.wait()
    raw_copies[1, b].start()
    raw_copies[3, b].start()
    lax.fori_loop(0, 16, gate_tile, 0)
    dispatch(1, a)
    dispatch(3, a)
    lax.fori_loop(0, FFW // BLOCK, turn, 0)
    for n, d in enumerate((0, 2)):
        pick_t[n] = pick[d].astype(F32).T.astype(BF)
    dispatch(0, g)
    dispatch(2, a)
    raw_copies[2, b].start()
    hidden_copy.start()
    weight_copies[b].start()
    weight_copies[g].start()
    dispatch(1, b)
    raw_copies[1, g].start()
    dispatch(3, b)
    raw_copies[3, g].start()
    dispatch(0, o)
    dispatch(2, b)
    raw_copies[2, g].start()
    raw_copies[3, o].start()
    weight_copies[a].wait_recv()
    for d in (0, 1, 3, 2):
        d_hidden(d, a)
    dispatch(3, g)
    dispatch(3, o)
    raw_copies[1, o].start()
    hidden_copy.wait_recv()
    partial(a)
    weight_copies[b].wait_recv()
    for d in (0, 1, 3, 2):
        d_hidden(d, b)
    partial(b)
    dispatch(1, g)
    raw_copies[2, o].start()
    dispatch(2, g)
    weight_copies[g].wait_recv()
    own_weight.wait()
    d_hidden(0, g)
    d_hidden(0, o)
    d_hidden(3, g)
    d_hidden(3, o)
    exchange(1)
    dispatch(1, o)
    d_hidden(1, g)
    d_hidden(2, g)
    partial(g)
    dispatch(2, o)
    d_hidden(1, o)
    exchange(0)
    d_hidden(2, o)
    send_back(1)
    partial(o)
    store = pltpu.make_async_copy(wts.at[o], parts.at[3], own_sem.at[6])
    store.start()
    collect(1, 0)
    collect(1, 1)
    send_back(0)
    for p in range(2, PARTS):
        collect(1, p)
    for p in range(PARTS):
        collect(0, p)

    store.wait()
    for copy in store_copies:
        copy.wait()
    for copy in list(part_copies.values()) + fin_copies:
        copy.wait_recv()
    sent = list(raw_copies.values()) + key_copies + list(weight_copies.values()) + [hidden_copy] + dh_copies
    sent += list(part_copies.values()) + fin_copies
    for unit in order[len(order) - OUTS :]:
        sent += x_copies[unit]
    for copies in ret_copies.values():
        sent += copies
    for copy in sent:
        copy.wait_send()


def shards(out_grad, expert_ids, stash_codes, stash_scale, down_weight):
    dma = pltpu.SemaphoreType.DMA
    hbm = pl.BlockSpec(memory_space=pl.ANY)
    vmem = pl.BlockSpec(memory_space=pltpu.VMEM)
    scratch = [
        pltpu.VMEM((4, 4, ROWS, FEAT), BF),
        pltpu.VMEM((OUTS, HALF, FEAT), BF),
        pltpu.VMEM((4, 4, HALF, FEAT), BF),
        pltpu.VMEM((4, FFW, FEAT), BF),
        pltpu.VMEM((2, FFW, SLOTS), BF),
        pltpu.VMEM((2, HALF, 2 * FFW), BF),
        pltpu.VMEM((4, HALF, FFW), F32),
        pltpu.VMEM((2, HALF, FFW), BF),
        pltpu.VMEM((2, HALF, FFW), BF),
        pltpu.VMEM((2, HALF, 2 * FFW), BF),
        pltpu.VMEM((2, HALF, 2 * FFW), BF),
        pltpu.VMEM((4, HALF, ROWS), BF),
        pltpu.VMEM((2, ROWS, HALF), BF),
        pltpu.VMEM((4, 8, ROWS), jnp.int32),
        pltpu.VMEM((2, ROWS, 2 * FFW), BF),
        pltpu.VMEM((16, 16, CAP), jnp.int32),
    ]
    for shape in [(4, 4), (4,), (4,), (16, 8), (1,), (2,), (3,), (2, PARTS, 8), (PARTS,)]:
        scratch += [dma(shape), dma(shape)]
    scratch += [dma((7,)), dma((16,)), dma((2, PARTS)), dma((PARTS,))]
    own_grad, far_grad, parts = pl.pallas_call(
        kernel,
        out_shape=(
            jax.ShapeDtypeStruct((ROWS, 2 * FFW), BF),
            jax.ShapeDtypeStruct((ROWS, 2 * FFW), BF),
            jax.ShapeDtypeStruct((4, FFW, FEAT), BF),
        ),
        in_specs=[hbm, vmem, hbm, hbm, hbm],
        out_specs=(hbm, hbm, hbm),
        scratch_shapes=scratch,
        compiler_params=pltpu.CompilerParams(
            collective_id=0, has_side_effects=True, vmem_limit_bytes=60 * 2**20
        ),
        name="expert_backward",
    )(out_grad, expert_ids.reshape(1, ROWS), stash_codes, jnp.swapaxes(stash_scale, 3, 4), down_weight)
    weight_grad = jnp.sum(parts.astype(F32), axis=0).astype(BF)[None]
    return own_grad + far_grad, weight_grad


def solution(mesh):
    placed = (
        P(("expert", "fsdp"), None),
        P(("expert", "fsdp"), None),
        P("expert", "fsdp", None, None, None),
        P("expert", "fsdp", None, None, None),
        P("expert", None, "fsdp"),
    )
    return jax.shard_map(
        shards,
        mesh=mesh,
        in_specs=placed,
        out_specs=(P(("expert", "fsdp"), None), P("expert", None, "fsdp")),
        check_vma=False,
    )
```

time: 535 us -> 192 us (0.36)
  Pallas kernels: 0 us -> 183 us
  waiting for transfers between devices: 165 us -> 0 us
  blocking collectives: 161 us -> 0 us
  local copies, waits for them, and re-layouts: 133 us -> 0 us
  matrix products: 41.6 us -> 0 us
  between operations: 14.1 us -> 0.64 us
  starting transfers between devices: 9.38 us -> 0 us
    pallas_call x0 -> x1, Pallas kernels: none -> 183 us  [shards(): pl.pallas_call(kernel, out_shape=(jax.ShapeDtypeStruct((ROWS, 2 * FFW), B...]
    all_to_all x1 -> x0, waiting for transfers between devices: 165 us -> none  [shards(): lax.all_to_all(outgoing, 'expert', split_axis=0, concat_axis=0, tiled=True)]
    all_to_all x1 -> x0, blocking collectives: 161 us -> none  [shards(): lax.all_to_all(returned_rows, 'expert', split_axis=0, concat_axis=0, tile...]
    scatter x1 -> x0, local copies, waits for them, and re-layouts: 96.3 us -> none  [shards(): outgoing = jnp.zeros((experts, capacity, features), out_grad.dtype).at[ex...]
    dot_general x2 -> x0, matrix products: 41.6 us -> none  [the longest x1 22 us: shards(): lax.dot_general(grad_rows, lax.all_gather(down_weight[0], 'fsdp', axis=1,...]
    unnamed x6 -> x0, local copies, waits for them, and re-layouts: 23.8 us -> none
    all_to_all x1 -> x0, starting transfers between devices: 9.12 us -> none  [shards(): lax.all_to_all(outgoing, 'expert', split_axis=0, concat_axis=0, tiled=True)]
    mul x1 -> x0, other arithmetic: 6.37 us -> none  [shards(): stash_values * factor[:, :, None]]
  transfers between devices with their start and end apart: 3 -> 0, of which waited for: 1 -> 0; matrix products, arithmetic and copies ran while one was open for 34% -> 0% of each run, Pallas kernels for 0% -> 0%
where the time goes in v2:
time: 192 us
  Pallas kernels  183 us (95%)
  other arithmetic  8.81 us (5%)
    pallas_call x1, Pallas kernels, shards(): pl.pallas_call(kernel, out_shape=(jax.ShapeDtypeStruct((ROWS, 2 * FFW), B...  183 us
    reduce_sum x1, other arithmetic, shards(): weight_grad = jnp.sum(parts.astype(F32), axis=0).astype(BF)[None]  5.9 us

profile of v2, /device:TPU:1, one launch (start us, length us, event | category | flops | bytes accessed | tf_op | source)
XLA Modules:
  0.0 192.3 jit_solution(4114814649419983953)
XLA Ops:
  0.6 182.8 %expert_backward.1 = (bf16[256,2048]{1,0:T(8,128)(2,1)}, bf16[256,2048]{1,0:T(8,128)(2,1)}, bf16[4,1024,896]{2,1,0:T(8,128)(2,1)}) custom-call(bf16[256,7168]{1,0:T(8,128)(2,1)} %grad.1, s32[1,256]{1,0:T(1,128)} %bitcast.5, bf16[1,1,16,48,2048]{4,3,2,1,0:T(8,128)(2,1)} %stash.1, s32[1,1,16,16,48]{4,3,2,1,0:T(8,128)} %bitcast.4, bf16[1,1024,896]{2,1,0:T(8,128)(2,1)} %weight.1), custom_call_target="tpu_custom_call" | custom-call | tf_op jit(solution)/shard_map/expert_backward/pallas_call | solution.py:374
  183.5 2.9 %add.3 = bf16[256,2048]{1,0:T(8,128)(2,1)} add(bf16[256,2048]{1,0:T(8,128)(2,1)} %get-tuple-element.5, bf16[256,2048]{1,0:T(8,128)(2,1)} %get-tuple-element.6) | non-fusion elementwise | flops 524288 | bytes 3145728 | tf_op jit(solution)/shard_map/add | solution.py:390
  186.4 5.9 %reduce_sum.12 = bf16[1024,896]{1,0:T(8,128)(2,1)} reduce(bf16[4,1024,896]{2,1,0:T(8,128)(2,1)} %get-tuple-element.7, bf16[]{:T(256)} %constant.2.clone.1), dimensions={0}, to_apply=%region_0.0 | reduce | flops 2752512 | bytes 9175042 | tf_op jit(solution)/shard_map/reduce_sum | solution.py:389

commit v3 on v2

--- a/solution.py
+++ b/solution.py
@@ -12,7 +12,7 @@
 FEAT = 896
 HALF = 8 * CAP
 SLOTS = 2 * HALF
-OUTS = 8
+OUTS = 6
 ORDER = (2, 1, 3, 0)
 PARTS = 4
 PCOLS = 2 * FFW // PARTS
@@ -23,10 +23,10 @@
 
 def kernel(
     grad, ids, stash, scale_in, weight,
-    own_grad, far_grad, parts,
-    raw, out, rows, wts, hidden, coef, dh, dh_out, dh_in, back, ret, pick, pick_t, keys, fin, scale,
+    own_grad, far_grad, weight_grad, parts,
+    raw, merged, out, rows, wts, hidden, coef, dh, dh_out, dh_in, back, ret, pick, pick_t, keys, fin, scale,
     raw_s, raw_r, key_s, key_r, w_s, w_r, x_s, x_r, hid_s, hid_r, dh_s, dh_r, part_s, part_r, ret_s, ret_r, fin_s, fin_r,
-    own_sem, stash_sem, self_sem, store_sem,
+    own_sem, other_sem, stash_sem, self_sem, store_sem, load_sem,
 ):
     e = lax.axis_index("expert")
     f = lax.axis_index("fsdp")
@@ -74,8 +74,12 @@
             pltpu.make_async_copy(stash.at[0, 0, g], back.at[s // 8, pl.ds((s % 8) * CAP, CAP)], stash_sem.at[s])
         )
     own_weight = pltpu.make_async_copy(weight.at[0], wts.at[0], own_sem.at[4])
+    other_rows = {
+        j: pltpu.make_async_copy(grad.at[:, columns(1 - zl, j)], merged.at[j], other_sem.at[j]) for j in ORDER
+    }
     for j in ORDER:
         own_rows[j].start()
+        other_rows[j].start()
     for copy in stash_copies:
         copy.start()
     own_weight.start()
@@ -101,17 +105,32 @@
             pick[d, k * CAP : (k + 1) * CAP, :] = jnp.where(key_of - base == place, 1.0, 0.0).astype(BF)
 
     make_pick(0)
+    near = jnp.broadcast_to(expert_of // 8 == zh, (8, ROWS)).astype(F32).T[:, 0:1] > 0.5
     pl.semaphore_wait(barrier, len(peers))
 
-    raw_copies = {
-        (d, j): remote(
-            grad.at[:, columns(1 - zl if d & 1 else zl, j)], raw.at[d, j], raw_s.at[d, j], raw_r.at[d, j], z_peer(d)
+    raw_copies = {}
+    for j in ORDER:
+        raw_copies[1, j] = remote(merged.at[j], raw.at[1, j], raw_s.at[1, j], raw_r.at[1, j], z_peer(1))
+        raw_copies[2, j] = remote(raw.at[1, j], raw.at[2, j], raw_s.at[2, j], raw_r.at[2, j], z_peer(3))
+        raw_copies[3, j] = remote(
+            grad.at[:, columns(1 - zl, j)], raw.at[3, j], raw_s.at[3, j], raw_r.at[3, j], z_peer(3)
         )
-        for d in (1, 2, 3)
-        for j in ORDER
-    }
+
+    def merge(j):
+        other_rows[j].wait()
+        own_rows[j].wait()
+
+        def tile(t, _):
+            at = pl.ds(pl.multiple_of(t * BLOCK, BLOCK), BLOCK)
+            merged[j, :, at] = jnp.where(near, merged[j, :, at].astype(F32), raw[0, j, :, at].astype(F32)).astype(BF)
+            return 0
+
+        lax.fori_loop(0, FEAT // BLOCK, tile, 0)
     key_copies = [remote(keys.at[0], keys.at[d], key_s.at[d], key_r.at[d], z_peer(d)) for d in (1, 2, 3)]
-    weight_copies = {j: remote(weight.at[0], wts.at[j], w_s.at[j], w_r.at[j], y_peer(-j)) for j in (1, 2, 3)}
+    weight_copies = {j: remote(weight.at[0], wts.at[j], w_s.at[j], w_r.at[j], y_peer(-j)) for j in (1, 3)}
+    upper, lower = pl.ds(0, FFW // 2), pl.ds(FFW // 2, FFW // 2)
+    weight_copies[0] = remote(wts.at[1, upper], wts.at[2, upper], w_s.at[0], w_r.at[0], y_peer(-1))
+    weight_copies[2] = remote(wts.at[3, lower], wts.at[2, lower], w_s.at[2], w_r.at[2], y_peer(1))
     hidden_copy = remote(hidden.at[0], hidden.at[1], hid_s.at[0], hid_r.at[0], z_peer(1))
     dh_copies = [remote(dh_out.at[zr], dh_in.at[zr], dh_s.at[zr], dh_r.at[zr], z_peer(1)) for zr in range(2)]
     part_copies = {
@@ -128,10 +147,10 @@
             for copy in x_copies[order[unit - OUTS]]:
                 copy.wait_send()
         order.append((d, j))
-        if d == 0:
-            own_rows[j].wait()
-        else:
+        if d:
             raw_copies[d, j].wait_recv()
+        if d == 1:
+            raw_copies[2, j].start()
 
         def tile(t, _):
             at = pl.ds(pl.multiple_of(t * 192, 192), 192)
@@ -253,76 +272,87 @@
             store_copies.append(copy)
         copy.start()
 
+    def collect_part(j):
+        part_copies[j].wait_recv()
+        part_copies[j].wait_send()
+        load = pltpu.make_async_copy(parts.at[j - 1], wts.at[j], load_sem.at[j])
+        load.start()
+        return load
+
     a, b, g, o = ORDER
     for copy in key_copies:
         copy.start()
-    for d in (1, 3, 2):
-        raw_copies[d, a].start()
-    weight_copies[a].start()
+    raw_copies[3, a].start()
+    weight_copies[1].start()
+    weight_copies[3].start()
+    merge(a)
+    raw_copies[1, a].start()
     dispatch(0, a)
+    merge(b)
+    raw_copies[1, b].start()
+    raw_copies[3, b].start()
     dispatch(0, b)
+    merge(g)
+    merge(o)
     for copy in key_copies:
         copy.wait_recv()
     for d in (1, 3, 2):
         make_pick(d)
     for copy in stash_copies:
         copy.wait()
-    raw_copies[1, b].start()
-    raw_copies[3, b].start()
     lax.fori_loop(0, 16, gate_tile, 0)
     dispatch(1, a)
     dispatch(3, a)
+    raw_copies[1, g].start()
+    raw_copies[3, g].start()
     lax.fori_loop(0, FFW // BLOCK, turn, 0)
+    hidden_copy.start()
     for n, d in enumerate((0, 2)):
         pick_t[n] = pick[d].astype(F32).T.astype(BF)
+    dispatch(2, a)
+    dispatch(1, b)
+    raw_copies[1, o].start()
+    dispatch(3, b)
+    raw_copies[3, o].start()
+    weight_copies[1].wait_recv()
+    weight_copies[0].start()
+    weight_copies[3].wait_recv()
+    weight_copies[2].start()
+    dispatch(2, b)
+    dispatch(1, g)
+    dispatch(3, g)
     dispatch(0, g)
-    dispatch(2, a)
-    raw_copies[2, b].start()
-    hidden_copy.start()
-    weight_copies[b].start()
-    weight_copies[g].start()
-    dispatch(1, b)
-    raw_copies[1, g].start()
-    dispatch(3, b)
-    raw_copies[3, g].start()
-    dispatch(0, o)
-    dispatch(2, b)
-    raw_copies[2, g].start()
-    raw_copies[3, o].start()
-    weight_copies[a].wait_recv()
+    weight_copies[0].wait_recv()
+    weight_copies[2].wait_recv()
     for d in (0, 1, 3, 2):
         d_hidden(d, a)
-    dispatch(3, g)
     dispatch(3, o)
-    raw_copies[1, o].start()
     hidden_copy.wait_recv()
     partial(a)
-    weight_copies[b].wait_recv()
+    dispatch(1, o)
     for d in (0, 1, 3, 2):
         d_hidden(d, b)
+    weight_copies[0].wait_send()
     partial(b)
-    dispatch(1, g)
-    raw_copies[2, o].start()
     dispatch(2, g)
-    weight_copies[g].wait_recv()
     own_weight.wait()
-    d_hidden(0, g)
-    d_hidden(0, o)
+    d_hidden(1, g)
     d_hidden(3, g)
     d_hidden(3, o)
     exchange(1)
-    dispatch(1, o)
-    d_hidden(1, g)
-    d_hidden(2, g)
-    partial(g)
+    dispatch(0, o)
     dispatch(2, o)
     d_hidden(1, o)
     exchange(0)
+    d_hidden(0, g)
+    d_hidden(2, g)
+    weight_copies[2].wait_send()
+    partial(g)
+    d_hidden(0, o)
     d_hidden(2, o)
     send_back(1)
     partial(o)
-    store = pltpu.make_async_copy(wts.at[o], parts.at[3], own_sem.at[6])
-    store.start()
+    loads = [collect_part(a)]
     collect(1, 0)
     collect(1, 1)
     send_back(0)
@@ -330,14 +360,29 @@
         collect(1, p)
     for p in range(PARTS):
         collect(0, p)
+    loads += [collect_part(b), collect_part(g)]
+    for load in loads:
+        load.wait()
+
+    def sum_tile(t, _):
+        at = pl.ds(pl.multiple_of(t * 64, 64), 64)
+        total = wts[0, at, :].astype(F32)
+        for j in range(1, 4):
+            total += wts[j, at, :].astype(F32)
+        wts[0, at, :] = total.astype(BF)
+        return 0
+
+    lax.fori_loop(0, FFW // 64, sum_tile, 0)
+    store = pltpu.make_async_copy(wts.at[0], weight_grad.at[0], own_sem.at[6])
+    store.start()
 
     store.wait()
     for copy in store_copies:
         copy.wait()
-    for copy in list(part_copies.values()) + fin_copies:
+    for copy in fin_copies:
         copy.wait_recv()
-    sent = list(raw_copies.values()) + key_copies + list(weight_copies.values()) + [hidden_copy] + dh_copies
-    sent += list(part_copies.values()) + fin_copies
+    sent = list(raw_copies.values()) + key_copies + [weight_copies[1], weight_copies[3]] + [hidden_copy] + dh_copies
+    sent += fin_copies
     for unit in order[len(order) - OUTS :]:
         sent += x_copies[unit]
     for copies in ret_copies.values():
@@ -352,6 +397,7 @@
     vmem = pl.BlockSpec(memory_space=pltpu.VMEM)
     scratch = [
         pltpu.VMEM((4, 4, ROWS, FEAT), BF),
+        pltpu.VMEM((4, ROWS, FEAT), BF),
         pltpu.VMEM((OUTS, HALF, FEAT), BF),
         pltpu.VMEM((4, 4, HALF, FEAT), BF),
         pltpu.VMEM((4, FFW, FEAT), BF),
@@ -370,23 +416,23 @@
     ]
     for shape in [(4, 4), (4,), (4,), (16, 8), (1,), (2,), (3,), (2, PARTS, 8), (PARTS,)]:
         scratch += [dma(shape), dma(shape)]
-    scratch += [dma((7,)), dma((16,)), dma((2, PARTS)), dma((PARTS,))]
-    own_grad, far_grad, parts = pl.pallas_call(
+    scratch += [dma((7,)), dma((4,)), dma((16,)), dma((2, PARTS)), dma((PARTS,)), dma((4,))]
+    own_grad, far_grad, weight_grad, _ = pl.pallas_call(
         kernel,
         out_shape=(
             jax.ShapeDtypeStruct((ROWS, 2 * FFW), BF),
             jax.ShapeDtypeStruct((ROWS, 2 * FFW), BF),
-            jax.ShapeDtypeStruct((4, FFW, FEAT), BF),
+            jax.ShapeDtypeStruct((1, FFW, FEAT), BF),
+            jax.ShapeDtypeStruct((3, FFW, FEAT), BF),
         ),
         in_specs=[hbm, vmem, hbm, hbm, hbm],
-        out_specs=(hbm, hbm, hbm),
+        out_specs=(hbm, hbm, hbm, hbm),
         scratch_shapes=scratch,
         compiler_params=pltpu.CompilerParams(
             collective_id=0, has_side_effects=True, vmem_limit_bytes=60 * 2**20
         ),
         name="expert_backward",
     )(out_grad, expert_ids.reshape(1, ROWS), stash_codes, jnp.swapaxes(stash_scale, 3, 4), down_weight)
-    weight_grad = jnp.sum(parts.astype(F32), axis=0).astype(BF)[None]
     return own_grad + far_grad, weight_grad
 
 

time: 192 us -> 183 us (0.953)
  other arithmetic: 8.81 us -> 3.04 us
  Pallas kernels: 183 us -> 178 us
    reduce_sum x1 -> x0, other arithmetic: 5.9 us -> none  [shards(): weight_grad = jnp.sum(parts.astype(F32), axis=0).astype(BF)[None]]
    pallas_call x1, Pallas kernels: 183 us -> 178 us  [shards(): pl.pallas_call(kernel, out_shape=(jax.ShapeDtypeStruct((ROWS, 2 * FFW), B...]
where the time goes in v3:
time: 183 us
  Pallas kernels  178 us (97%)
  other arithmetic  3.04 us (2%)
    pallas_call x1, Pallas kernels, shards(): pl.pallas_call(kernel, out_shape=(jax.ShapeDtypeStruct((ROWS, 2 * FFW), B...  178 us

profile of v3, /device:TPU:1, one launch (start us, length us, event | category | flops | bytes accessed | tf_op | source)
XLA Modules:
  0.0 183.2 jit_solution(11124962241009653712)
XLA Ops:
  0.6 178.3 %expert_backward.1 = (bf16[256,2048]{1,0:T(8,128)(2,1)}, bf16[256,2048]{1,0:T(8,128)(2,1)}, bf16[1,1024,896]{2,1,0:T(8,128)(2,1)}, bf16[3,1024,896]{2,1,0:T(8,128)(2,1)}) custom-call(bf16[256,7168]{1,0:T(8,128)(2,1)} %grad.1, s32[1,256]{1,0:T(1,128)} %bitcast.3, bf16[1,1,16,48,2048]{4,3,2,1,0:T(8,128)(2,1)} %stash.1, s32[1,1,16,16,48]{4,3,2,1,0:T(8,128)} %bitcast.2, ...), custom_call_target="tpu_custom_call" | custom-call | tf_op jit(solution)/shard_map/expert_backward/pallas_call | solution.py:420
  178.9 0.0 copy-start
  178.9 3.0 %add.3 = bf16[256,2048]{1,0:T(8,128)(2,1)} add(bf16[256,2048]{1,0:T(8,128)(2,1)} %get-tuple-element.5, bf16[256,2048]{1,0:T(8,128)(2,1)} %get-tuple-element.6) | non-fusion elementwise | flops 524288 | bytes 3145728 | tf_op jit(solution)/shard_map/add | solution.py:436
  182.0 0.0 copy-done
  182.0 1.2 copy.8
Async XLA Ops:
  178.9 3.1 %copy-start = (bf16[1,1024,896]{2,1,0:T(8,128)(2,1)S(1)}, bf16[1,1024,896]{2,1,0:T(8,128)(2,1)}, u32[]{:S(2)}) copy-start(bf16[1,1024,896]{2,1,0:T(8,128)(2,1)} %get-tuple-element.11) | copy-start | bytes 5505028

commit v4 on v3

--- a/solution.py
+++ b/solution.py
@@ -13,6 +13,7 @@
 HALF = 8 * CAP
 SLOTS = 2 * HALF
 OUTS = 6
+PLACE = (0, 2, 1, 3)
 ORDER = (2, 1, 3, 0)
 PARTS = 4
 PCOLS = 2 * FFW // PARTS
@@ -24,8 +25,8 @@
 def kernel(
     grad, ids, stash, scale_in, weight,
     own_grad, far_grad, weight_grad, parts,
-    raw, merged, out, rows, wts, hidden, coef, dh, dh_out, dh_in, back, ret, pick, pick_t, keys, fin, scale,
-    raw_s, raw_r, key_s, key_r, w_s, w_r, x_s, x_r, hid_s, hid_r, dh_s, dh_r, part_s, part_r, ret_s, ret_r, fin_s, fin_r,
+    raw, merged, out, rows, wts, far_part, far_in, hidden, coef, dh, dh_out, dh_in, back, ret, pick, pick_t, keys, fin, scale,
+    raw_s, raw_r, key_s, key_r, w_s, w_r, x_s, x_r, hid_s, hid_r, dh_s, dh_r, far_s, far_r, part_s, part_r, ret_s, ret_r, fin_s, fin_r,
     own_sem, other_sem, stash_sem, self_sem, store_sem, load_sem,
 ):
     e = lax.axis_index("expert")
@@ -65,6 +66,9 @@
 
     own_rows = {
         j: pltpu.make_async_copy(grad.at[:, columns(zl, j)], raw.at[0, j], own_sem.at[j]) for j in ORDER
+    }
+    other_rows = {
+        j: pltpu.make_async_copy(grad.at[:, columns(1 - zl, j)], merged.at[j], other_sem.at[j]) for j in ORDER
     }
     stash_copies = [pltpu.make_async_copy(scale_in.at[0, 0], scale, own_sem.at[5])]
     for s in range(16):
@@ -74,15 +78,9 @@
             pltpu.make_async_copy(stash.at[0, 0, g], back.at[s // 8, pl.ds((s % 8) * CAP, CAP)], stash_sem.at[s])
         )
     own_weight = pltpu.make_async_copy(weight.at[0], wts.at[0], own_sem.at[4])
-    other_rows = {
-        j: pltpu.make_async_copy(grad.at[:, columns(1 - zl, j)], merged.at[j], other_sem.at[j]) for j in ORDER
-    }
     for j in ORDER:
         own_rows[j].start()
         other_rows[j].start()
-    for copy in stash_copies:
-        copy.start()
-    own_weight.start()
 
     expert_of = ids[...]
     same = lax.broadcasted_iota(jnp.int32, (16, ROWS), 0) == expert_of
@@ -106,7 +104,6 @@
 
     make_pick(0)
     near = jnp.broadcast_to(expert_of // 8 == zh, (8, ROWS)).astype(F32).T[:, 0:1] > 0.5
-    pl.semaphore_wait(barrier, len(peers))
 
     raw_copies = {}
     for j in ORDER:
@@ -116,9 +113,16 @@
             grad.at[:, columns(1 - zl, j)], raw.at[3, j], raw_s.at[3, j], raw_r.at[3, j], z_peer(3)
         )
 
+    loaded = []
+
+    def own_ready(j):
+        if j not in loaded:
+            loaded.append(j)
+            own_rows[j].wait()
+
     def merge(j):
         other_rows[j].wait()
-        own_rows[j].wait()
+        own_ready(j)
 
         def tile(t, _):
             at = pl.ds(pl.multiple_of(t * BLOCK, BLOCK), BLOCK)
@@ -131,16 +135,20 @@
     upper, lower = pl.ds(0, FFW // 2), pl.ds(FFW // 2, FFW // 2)
     weight_copies[0] = remote(wts.at[1, upper], wts.at[2, upper], w_s.at[0], w_r.at[0], y_peer(-1))
     weight_copies[2] = remote(wts.at[3, lower], wts.at[2, lower], w_s.at[2], w_r.at[2], y_peer(1))
-    hidden_copy = remote(hidden.at[0], hidden.at[1], hid_s.at[0], hid_r.at[0], z_peer(1))
+    hidden_copy = remote(hidden.at[:, pl.ds(0, SLOTS)], hidden.at[:, pl.ds(SLOTS, SLOTS)], hid_s.at[0], hid_r.at[0], z_peer(1))
     dh_copies = [remote(dh_out.at[zr], dh_in.at[zr], dh_s.at[zr], dh_r.at[zr], z_peer(1)) for zr in range(2)]
+    far_copies = [
+        remote(far_part.at[half], far_in.at[n], far_s.at[n], far_r.at[n], y_peer(1 - 2 * n))
+        for n, half in enumerate((upper, lower))
+    ]
     part_copies = {
-        j: remote(wts.at[j], parts.at[j - 1], part_s.at[j - 1], part_r.at[j - 1], y_peer(j)) for j in (1, 2, 3)
+        j: remote(wts.at[j], parts.at[j // 2], part_s.at[j // 2], part_r.at[j // 2], y_peer(j)) for j in (1, 3)
     }
 
     x_copies = {}
     order = []
 
-    def dispatch(d, j):
+    def put(d, j):
         unit = len(order)
         into = unit % OUTS
         if unit >= OUTS:
@@ -149,6 +157,8 @@
         order.append((d, j))
         if d:
             raw_copies[d, j].wait_recv()
+        else:
+            own_ready(j)
         if d == 1:
             raw_copies[2, j].start()
 
@@ -158,12 +168,18 @@
             return 0
 
         lax.fori_loop(0, 2, tile, 0)
-        rows[d, j, 0:CAP, :] = out[into, 0:CAP, :]
+        rows[j, PLACE[d], 0:CAP, :] = out[into, 0:CAP, :]
+
+    def dispatch(d, j):
+        if (d, j) not in order:
+            put(d, j)
+        unit = order.index((d, j))
+        into = unit % OUTS
         x_copies[d, j] = []
         for k in range(1, 8):
             block = pl.ds(k * CAP, CAP)
             copy = remote(
-                out.at[into, block, :], rows.at[d, j, block, :], x_s.at[unit, k], x_r.at[unit, k], x_peer(k, 1)
+                out.at[into, block, :], rows.at[j, PLACE[d], block, :], x_s.at[unit, k], x_r.at[unit, k], x_peer(k, 1)
             )
             copy.start()
             x_copies[d, j].append(copy)
@@ -190,42 +206,59 @@
     def turn(b, _):
         at = pl.ds(pl.multiple_of(b * BLOCK, BLOCK), BLOCK)
         for zr in range(2):
-            hidden[0, at, zr * HALF : (zr + 1) * HALF] = dh_out[zr, :, at].T
+            hidden[at, zr * HALF : (zr + 1) * HALF] = dh_out[zr, :, at].T
         return 0
 
+    def arrived(j, sources):
+        for d in sources:
+            for copy in x_copies[d, j]:
+                copy.wait_recv()
+
     def d_hidden(d, j):
-        for copy in x_copies[d, j]:
-            copy.wait_recv()
-
+        arrived(j, (d,))
+
+        def tile(n, _):
+            at = pl.ds(pl.multiple_of(n * 256, 256), 256)
+            dh[PLACE[d], :, at] += lax.dot_general(
+                rows[j, PLACE[d]], wts[j, at, :], (((1,), (1,)), ((), ())), preferred_element_type=F32
+            )
+            return 0
+
+        lax.fori_loop(0, FFW // 256, tile, 0)
+
+    def d_hidden_all(j, start):
         def tile(n, _):
             at = pl.ds(pl.multiple_of(n * 256, 256), 256)
             term = lax.dot_general(
-                rows[d, j], wts[j, at, :], (((1,), (1,)), ((), ())), preferred_element_type=F32
-            )
-            if j == ORDER[0]:
-                dh[d, :, at] = term
-            else:
-                dh[d, :, at] += term
+                rows[j].reshape(2 * SLOTS, FEAT), wts[j, at, :], (((1,), (1,)), ((), ())), preferred_element_type=F32
+            ).reshape(4, HALF, 256)
+            dh[:, :, at] = term if start else dh[:, :, at] + term
             return 0
 
         lax.fori_loop(0, FFW // 256, tile, 0)
 
     def partial(j):
-        def tile(m, _):
-            at = pl.ds(pl.multiple_of(m * 256, 256), 256)
-            term = jnp.dot(hidden[0, at, 0:HALF], rows[0, j], preferred_element_type=F32)
-            term += jnp.dot(hidden[0, at, HALF:SLOTS], rows[2, j], preferred_element_type=F32)
-            term += jnp.dot(hidden[1, at, 0:HALF], rows[1, j], preferred_element_type=F32)
-            term += jnp.dot(hidden[1, at, HALF:SLOTS], rows[3, j], preferred_element_type=F32)
-            wts[j, at, :] = term.astype(BF)
-            return 0
-
-        lax.fori_loop(0, FFW // 256, tile, 0)
-        if j:
+        into = far_part if j == 2 else wts.at[j]
+        for n in range(2):
+
+            def tile(m, _, n=n):
+                at = pl.ds(pl.multiple_of(n * (FFW // 2) + m * 256, 256), 256)
+                term = jnp.dot(hidden[at, :], rows[j].reshape(2 * SLOTS, FEAT), preferred_element_type=F32)
+                if j == 1 + 2 * n:
+                    term += far_in[n, pl.ds(pl.multiple_of(m * 256, 256), 256), :].astype(F32)
+                into[at, :] = term.astype(BF)
+                return 0
+
+            if j == 1 + 2 * n:
+                far_copies[n].wait_recv()
+            lax.fori_loop(0, 2, tile, 0)
+            if j == 2:
+                far_copies[n].start()
+        if j in (1, 3):
             part_copies[j].start()
 
     def exchange(zr):
-        dh_out[zr] = dh[1 + 2 * zr].astype(BF)
+        dh_out[zr] = dh[PLACE[1 + 2 * zr]].astype(BF)
         dh_copies[zr].start()
 
     ret_copies, self_copies, fin_copies, store_copies = {}, {}, [], []
@@ -238,7 +271,7 @@
 
             def back_tile(k, _, cols=cols, dh_cols=dh_cols):
                 at = pl.ds(pl.multiple_of(k * CAP, CAP), CAP)
-                total = dh[2 * zr, at, dh_cols] + dh_in[zr, at, dh_cols].astype(F32)
+                total = dh[PLACE[2 * zr], at, dh_cols] + dh_in[zr, at, dh_cols].astype(F32)
                 back[zr, at, cols] = (total * coef[zr, at, cols].astype(F32)).astype(BF)
                 return 0
 
@@ -275,25 +308,30 @@
     def collect_part(j):
         part_copies[j].wait_recv()
         part_copies[j].wait_send()
-        load = pltpu.make_async_copy(parts.at[j - 1], wts.at[j], load_sem.at[j])
+        load = pltpu.make_async_copy(parts.at[j // 2], wts.at[j], load_sem.at[j])
         load.start()
         return load
 
     a, b, g, o = ORDER
+    put(0, a)
+    merge(a)
+    pl.semaphore_wait(barrier, len(peers))
+    dispatch(0, a)
+    raw_copies[1, a].start()
+    raw_copies[3, a].start()
     for copy in key_copies:
         copy.start()
-    raw_copies[3, a].start()
     weight_copies[1].start()
     weight_copies[3].start()
-    merge(a)
-    raw_copies[1, a].start()
-    dispatch(0, a)
     merge(b)
     raw_copies[1, b].start()
     raw_copies[3, b].start()
     dispatch(0, b)
     merge(g)
     merge(o)
+    for copy in stash_copies:
+        copy.start()
+    own_weight.start()
     for copy in key_copies:
         copy.wait_recv()
     for d in (1, 3, 2):
@@ -303,7 +341,6 @@
     lax.fori_loop(0, 16, gate_tile, 0)
     dispatch(1, a)
     dispatch(3, a)
-    raw_copies[1, g].start()
     raw_copies[3, g].start()
     lax.fori_loop(0, FFW // BLOCK, turn, 0)
     hidden_copy.start()
@@ -311,63 +348,62 @@
         pick_t[n] = pick[d].astype(F32).T.astype(BF)
     dispatch(2, a)
     dispatch(1, b)
-    raw_copies[1, o].start()
     dispatch(3, b)
     raw_copies[3, o].start()
+    dispatch(2, b)
+    raw_copies[1, g].start()
     weight_copies[1].wait_recv()
     weight_copies[0].start()
     weight_copies[3].wait_recv()
     weight_copies[2].start()
-    dispatch(2, b)
+    dispatch(0, g)
+    dispatch(3, g)
+    dispatch(3, o)
+    raw_copies[1, o].start()
+    arrived(a, (0, 1, 3, 2))
+    hidden_copy.wait_recv()
+    partial(a)
     dispatch(1, g)
-    dispatch(3, g)
-    dispatch(0, g)
+    arrived(b, (0, 1, 3, 2))
+    d_hidden_all(b, True)
+    dispatch(2, g)
     weight_copies[0].wait_recv()
     weight_copies[2].wait_recv()
-    for d in (0, 1, 3, 2):
-        d_hidden(d, a)
-    dispatch(3, o)
-    hidden_copy.wait_recv()
-    partial(a)
-    dispatch(1, o)
-    for d in (0, 1, 3, 2):
-        d_hidden(d, b)
-    weight_copies[0].wait_send()
-    partial(b)
-    dispatch(2, g)
+    d_hidden_all(a, False)
     own_weight.wait()
-    d_hidden(1, g)
     d_hidden(3, g)
     d_hidden(3, o)
     exchange(1)
+    dispatch(1, o)
+    dispatch(2, o)
     dispatch(0, o)
-    dispatch(2, o)
-    d_hidden(1, o)
-    exchange(0)
+    weight_copies[0].wait_send()
+    partial(b)
     d_hidden(0, g)
+    d_hidden(1, g)
     d_hidden(2, g)
     weight_copies[2].wait_send()
     partial(g)
-    d_hidden(0, o)
+    d_hidden(1, o)
+    exchange(0)
     d_hidden(2, o)
     send_back(1)
+    d_hidden(0, o)
+    collect(1, 0)
+    send_back(0)
     partial(o)
-    loads = [collect_part(a)]
-    collect(1, 0)
-    collect(1, 1)
-    send_back(0)
-    for p in range(2, PARTS):
+    for p in range(1, PARTS):
         collect(1, p)
-    for p in range(PARTS):
+    for p in range(PARTS - 1):
         collect(0, p)
-    loads += [collect_part(b), collect_part(g)]
+    loads = [collect_part(b), collect_part(g)]
     for load in loads:
         load.wait()
 
     def sum_tile(t, _):
         at = pl.ds(pl.multiple_of(t * 64, 64), 64)
         total = wts[0, at, :].astype(F32)
-        for j in range(1, 4):
+        for j in (1, 3):
             total += wts[j, at, :].astype(F32)
         wts[0, at, :] = total.astype(BF)
         return 0
@@ -375,6 +411,7 @@
     lax.fori_loop(0, FFW // 64, sum_tile, 0)
     store = pltpu.make_async_copy(wts.at[0], weight_grad.at[0], own_sem.at[6])
     store.start()
+    collect(0, PARTS - 1)
 
     store.wait()
     for copy in store_copies:
@@ -382,13 +419,65 @@
     for copy in fin_copies:
         copy.wait_recv()
     sent = list(raw_copies.values()) + key_copies + [weight_copies[1], weight_copies[3]] + [hidden_copy] + dh_copies
-    sent += fin_copies
+    sent += fin_copies + far_copies
     for unit in order[len(order) - OUTS :]:
         sent += x_copies[unit]
     for copies in ret_copies.values():
         sent += copies
     for copy in sent:
         copy.wait_send()
+
+
+def last(own_ref, far_ref, weight_ref, in_grad, weight_grad, own, far, share, sems):
+    rows, high = ROWS // 4, FFW // 4
+    loads, stores = [], []
+    for t in range(4):
+        at, part = pl.ds(t * rows, rows), pl.ds(t * high, high)
+        loads.append(
+            [
+                pltpu.make_async_copy(own_ref.at[at], own.at[at], sems.at[0, t]),
+                pltpu.make_async_copy(far_ref.at[at], far.at[at], sems.at[1, t]),
+                pltpu.make_async_copy(weight_ref.at[0, part], share.at[part], sems.at[2, t]),
+            ]
+        )
+        stores.append(
+            [
+                pltpu.make_async_copy(own.at[at], in_grad.at[at], sems.at[3, t]),
+                pltpu.make_async_copy(share.at[part], weight_grad.at[0, part], sems.at[4, t]),
+            ]
+        )
+        for load in loads[t]:
+            load.start()
+    for t in range(4):
+        at = pl.ds(t * rows, rows)
+        for load in loads[t]:
+            load.wait()
+        own[at, :] = own[at, :] + far[at, :]
+        for store in stores[t]:
+            store.start()
+    for group in stores:
+        for store in group:
+            store.wait()
+
+
+def finish(own_grad, far_grad, weight_grad):
+    hbm = pl.BlockSpec(memory_space=pl.ANY)
+    return pl.pallas_call(
+        last,
+        out_shape=(
+            jax.ShapeDtypeStruct(own_grad.shape, BF),
+            jax.ShapeDtypeStruct(weight_grad.shape, BF),
+        ),
+        in_specs=[hbm, hbm, hbm],
+        out_specs=(hbm, hbm),
+        scratch_shapes=[
+            pltpu.VMEM((ROWS, 2 * FFW), BF),
+            pltpu.VMEM((ROWS, 2 * FFW), BF),
+            pltpu.VMEM((FFW, FEAT), BF),
+            pltpu.SemaphoreType.DMA((5, 4)),
+        ],
+        name="finish",
+    )(own_grad, far_grad, weight_grad)
 
 
 def shards(out_grad, expert_ids, stash_codes, stash_scale, down_weight):
@@ -401,7 +490,9 @@
         pltpu.VMEM((OUTS, HALF, FEAT), BF),
         pltpu.VMEM((4, 4, HALF, FEAT), BF),
         pltpu.VMEM((4, FFW, FEAT), BF),
-        pltpu.VMEM((2, FFW, SLOTS), BF),
+        pltpu.VMEM((FFW, FEAT), BF),
+        pltpu.VMEM((2, FFW // 2, FEAT), BF),
+        pltpu.VMEM((FFW, 2 * SLOTS), BF),
         pltpu.VMEM((2, HALF, 2 * FFW), BF),
         pltpu.VMEM((4, HALF, FFW), F32),
         pltpu.VMEM((2, HALF, FFW), BF),
@@ -414,7 +505,7 @@
         pltpu.VMEM((2, ROWS, 2 * FFW), BF),
         pltpu.VMEM((16, 16, CAP), jnp.int32),
     ]
-    for shape in [(4, 4), (4,), (4,), (16, 8), (1,), (2,), (3,), (2, PARTS, 8), (PARTS,)]:
+    for shape in [(4, 4), (4,), (4,), (16, 8), (1,), (2,), (2,), (2,), (2, PARTS, 8), (PARTS,)]:
         scratch += [dma(shape), dma(shape)]
     scratch += [dma((7,)), dma((4,)), dma((16,)), dma((2, PARTS)), dma((PARTS,)), dma((4,))]
     own_grad, far_grad, weight_grad, _ = pl.pallas_call(
@@ -423,7 +514,7 @@
             jax.ShapeDtypeStruct((ROWS, 2 * FFW), BF),
             jax.ShapeDtypeStruct((ROWS, 2 * FFW), BF),
             jax.ShapeDtypeStruct((1, FFW, FEAT), BF),
-            jax.ShapeDtypeStruct((3, FFW, FEAT), BF),
+            jax.ShapeDtypeStruct((2, FFW, FEAT), BF),
         ),
         in_specs=[hbm, vmem, hbm, hbm, hbm],
         out_specs=(hbm, hbm, hbm, hbm),
@@ -433,7 +524,7 @@
         ),
         name="expert_backward",
     )(out_grad, expert_ids.reshape(1, ROWS), stash_codes, jnp.swapaxes(stash_scale, 3, 4), down_weight)
-    return own_grad + far_grad, weight_grad
+    return finish(own_grad, far_grad, weight_grad)
 
 
 def solution(mesh):

time: 183 us -> 178 us (0.973)
  other arithmetic: 3.04 us -> 0 us
    pallas_call x1, Pallas kernels: 178 us -> 174 us  [shards(): pl.pallas_call(kernel, out_shape=(jax.ShapeDtypeStruct((ROWS, 2 * FFW), B...]
    pallas_call x0 -> x1, Pallas kernels: none -> 3.12 us  [finish(): pl.pallas_call(last, out_shape=(jax.ShapeDtypeStruct(own_grad.shape, BF),...]
    add x1 -> x0, other arithmetic: 3.04 us -> none  [shards(): return (own_grad + far_grad, weight_grad)]
where the time goes in v4:
time: 178 us
  Pallas kernels  177 us (99%)
    pallas_call x1, Pallas kernels, shards(): pl.pallas_call(kernel, out_shape=(jax.ShapeDtypeStruct((ROWS, 2 * FFW), B...  174 us

profile of v4, /device:TPU:1, one launch (start us, length us, event | category | flops | bytes accessed | tf_op | source)
XLA Modules:
  0.0 178.1 jit_solution(10889572734010125829)
XLA Ops:
  0.6 174.2 %expert_backward.1 = (bf16[256,2048]{1,0:T(8,128)(2,1)}, bf16[256,2048]{1,0:T(8,128)(2,1)}, bf16[1,1024,896]{2,1,0:T(8,128)(2,1)}, bf16[2,1024,896]{2,1,0:T(8,128)(2,1)}) custom-call(bf16[256,7168]{1,0:T(8,128)(2,1)} %grad.1, s32[1,256]{1,0:T(1,128)} %bitcast.3, bf16[1,1,16,48,2048]{4,3,2,1,0:T(8,128)(2,1)} %stash.1, s32[1,1,16,16,48]{4,3,2,1,0:T(8,128)} %bitcast.2, ...), custom_call_target="tpu_custom_call" | custom-call | tf_op jit(solution)/shard_map/expert_backward/pallas_call | solution.py:511
  174.8 3.1 %finish.1 = (bf16[256,2048]{1,0:T(8,128)(2,1)}, bf16[1,1024,896]{2,1,0:T(8,128)(2,1)}) custom-call(bf16[256,2048]{1,0:T(8,128)(2,1)} %get-tuple-element.5.own_ref, bf16[256,2048]{1,0:T(8,128)(2,1)} %get-tuple-element.6.far_ref, bf16[1,1024,896]{2,1,0:T(8,128)(2,1)} %get-tuple-element.7.weight_ref), custom_call_target="tpu_custom_call" | custom-call | tf_op jit(solution)/shard_map/finish/pallas_call | solution.py:465

commit v5 on v4

--- a/solution.py
+++ b/solution.py
@@ -314,23 +314,24 @@
 
     a, b, g, o = ORDER
     put(0, a)
-    merge(a)
     pl.semaphore_wait(barrier, len(peers))
     dispatch(0, a)
-    raw_copies[1, a].start()
     raw_copies[3, a].start()
     for copy in key_copies:
         copy.start()
+    merge(a)
+    raw_copies[1, a].start()
     weight_copies[1].start()
     weight_copies[3].start()
     merge(b)
     raw_copies[1, b].start()
     raw_copies[3, b].start()
     dispatch(0, b)
+    dispatch(0, g)
+    for copy in stash_copies:
+        copy.start()
     merge(g)
     merge(o)
-    for copy in stash_copies:
-        copy.start()
     own_weight.start()
     for copy in key_copies:
         copy.wait_recv()
@@ -356,7 +357,6 @@
     weight_copies[0].start()
     weight_copies[3].wait_recv()
     weight_copies[2].start()
-    dispatch(0, g)
     dispatch(3, g)
     dispatch(3, o)
     raw_copies[1, o].start()

time: 178 us -> 173 us (0.972)
  Pallas kernels: 177 us -> 173 us
    pallas_call x1, Pallas kernels: 174 us -> 169 us  [shards(): pl.pallas_call(kernel, out_shape=(jax.ShapeDtypeStruct((ROWS, 2 * FFW), B...]
where the time goes in v5:
time: 173 us
  Pallas kernels  173 us (100%)
    pallas_call x1, Pallas kernels, shards(): pl.pallas_call(kernel, out_shape=(jax.ShapeDtypeStruct((ROWS, 2 * FFW), B...  169 us

profile of v5, /device:TPU:1, one launch (start us, length us, event | category | flops | bytes accessed | tf_op | source)
XLA Modules:
  0.0 173.3 jit_solution(6284617309036932515)
XLA Ops:
  0.6 169.4 %expert_backward.1 = (bf16[256,2048]{1,0:T(8,128)(2,1)}, bf16[256,2048]{1,0:T(8,128)(2,1)}, bf16[1,1024,896]{2,1,0:T(8,128)(2,1)}, bf16[2,1024,896]{2,1,0:T(8,128)(2,1)}) custom-call(bf16[256,7168]{1,0:T(8,128)(2,1)} %grad.1, s32[1,256]{1,0:T(1,128)} %bitcast.3, bf16[1,1,16,48,2048]{4,3,2,1,0:T(8,128)(2,1)} %stash.1, s32[1,1,16,16,48]{4,3,2,1,0:T(8,128)} %bitcast.2, ...), custom_call_target="tpu_custom_call" | custom-call | tf_op jit(solution)/shard_map/expert_backward/pallas_call | solution.py:511
  170.0 3.1 %finish.1 = (bf16[256,2048]{1,0:T(8,128)(2,1)}, bf16[1,1024,896]{2,1,0:T(8,128)(2,1)}) custom-call(bf16[256,2048]{1,0:T(8,128)(2,1)} %get-tuple-element.5.own_ref, bf16[256,2048]{1,0:T(8,128)(2,1)} %get-tuple-element.6.far_ref, bf16[1,1024,896]{2,1,0:T(8,128)(2,1)} %get-tuple-element.7.weight_ref), custom_call_target="tpu_custom_call" | custom-call | tf_op jit(solution)/shard_map/finish/pallas_call | solution.py:465

commit v6 on v5

--- a/solution.py
+++ b/solution.py
@@ -27,7 +27,7 @@
     own_grad, far_grad, weight_grad, parts,
     raw, merged, out, rows, wts, far_part, far_in, hidden, coef, dh, dh_out, dh_in, back, ret, pick, pick_t, keys, fin, scale,
     raw_s, raw_r, key_s, key_r, w_s, w_r, x_s, x_r, hid_s, hid_r, dh_s, dh_r, far_s, far_r, part_s, part_r, ret_s, ret_r, fin_s, fin_r,
-    own_sem, other_sem, stash_sem, self_sem, store_sem, load_sem,
+    own_sem, other_sem, stash_sem, self_sem, load_sem,
 ):
     e = lax.axis_index("expert")
     f = lax.axis_index("fsdp")
@@ -261,7 +261,7 @@
         dh_out[zr] = dh[PLACE[1 + 2 * zr]].astype(BF)
         dh_copies[zr].start()
 
-    ret_copies, self_copies, fin_copies, store_copies = {}, {}, [], []
+    ret_copies, self_copies, fin_copies = {}, {}, []
 
     def send_back(zr):
         dh_copies[zr].wait_recv()
@@ -296,14 +296,14 @@
         self_copies[zr, p].wait()
         for copy in ret_copies[zr, p]:
             copy.wait_recv()
-        fin[zr, :, cols] = jnp.dot(pick_t[zr], ret[zr, :, cols], preferred_element_type=F32).astype(BF)
+        got = jnp.dot(pick_t[zr], ret[zr, :, cols], preferred_element_type=F32).astype(BF)
         if zr:
-            copy = remote(fin.at[1, :, cols], far_grad.at[:, cols], fin_s.at[p], fin_r.at[p], z_peer(2))
+            fin[:, cols] = got
+            copy = remote(fin.at[:, cols], far_grad.at[:, cols], fin_s.at[p], fin_r.at[p], z_peer(2))
+            copy.start()
             fin_copies.append(copy)
         else:
-            copy = pltpu.make_async_copy(fin.at[0, :, cols], own_grad.at[:, cols], store_sem.at[p])
-            store_copies.append(copy)
-        copy.start()
+            own_grad[:, cols] = got
 
     def collect_part(j):
         part_copies[j].wait_recv()
@@ -405,17 +405,11 @@
         total = wts[0, at, :].astype(F32)
         for j in (1, 3):
             total += wts[j, at, :].astype(F32)
-        wts[0, at, :] = total.astype(BF)
+        weight_grad[0, at, :] = total.astype(BF)
         return 0
 
     lax.fori_loop(0, FFW // 64, sum_tile, 0)
-    store = pltpu.make_async_copy(wts.at[0], weight_grad.at[0], own_sem.at[6])
-    store.start()
     collect(0, PARTS - 1)
-
-    store.wait()
-    for copy in store_copies:
-        copy.wait()
     for copy in fin_copies:
         copy.wait_recv()
     sent = list(raw_copies.values()) + key_copies + [weight_copies[1], weight_copies[3]] + [hidden_copy] + dh_copies
@@ -428,54 +422,38 @@
         copy.wait_send()
 
 
-def last(own_ref, far_ref, weight_ref, in_grad, weight_grad, own, far, share, sems):
-    rows, high = ROWS // 4, FFW // 4
-    loads, stores = [], []
-    for t in range(4):
-        at, part = pl.ds(t * rows, rows), pl.ds(t * high, high)
-        loads.append(
-            [
-                pltpu.make_async_copy(own_ref.at[at], own.at[at], sems.at[0, t]),
-                pltpu.make_async_copy(far_ref.at[at], far.at[at], sems.at[1, t]),
-                pltpu.make_async_copy(weight_ref.at[0, part], share.at[part], sems.at[2, t]),
-            ]
-        )
-        stores.append(
-            [
-                pltpu.make_async_copy(own.at[at], in_grad.at[at], sems.at[3, t]),
-                pltpu.make_async_copy(share.at[part], weight_grad.at[0, part], sems.at[4, t]),
-            ]
-        )
-        for load in loads[t]:
-            load.start()
+def last(own, far, share, in_grad, weight_grad, total, sems):
+    rows = ROWS // 4
+    out = pltpu.make_async_copy(share, weight_grad, sems.at[4])
+    out.start()
+    stores = []
     for t in range(4):
         at = pl.ds(t * rows, rows)
-        for load in loads[t]:
-            load.wait()
-        own[at, :] = own[at, :] + far[at, :]
-        for store in stores[t]:
-            store.start()
-    for group in stores:
-        for store in group:
-            store.wait()
+        total[at, :] = own[at, :] + far[at, :]
+        store = pltpu.make_async_copy(total.at[at], in_grad.at[at], sems.at[t])
+        store.start()
+        stores.append(store)
+    for store in stores:
+        store.wait()
+    out.wait()
 
 
 def finish(own_grad, far_grad, weight_grad):
     hbm = pl.BlockSpec(memory_space=pl.ANY)
+    vmem = pl.BlockSpec(memory_space=pltpu.VMEM)
     return pl.pallas_call(
         last,
         out_shape=(
             jax.ShapeDtypeStruct(own_grad.shape, BF),
             jax.ShapeDtypeStruct(weight_grad.shape, BF),
         ),
-        in_specs=[hbm, hbm, hbm],
+        in_specs=[vmem, vmem, vmem],
         out_specs=(hbm, hbm),
         scratch_shapes=[
             pltpu.VMEM((ROWS, 2 * FFW), BF),
-            pltpu.VMEM((ROWS, 2 * FFW), BF),
-            pltpu.VMEM((FFW, FEAT), BF),
-            pltpu.SemaphoreType.DMA((5, 4)),
+            pltpu.SemaphoreType.DMA((5,)),
         ],
+        compiler_params=pltpu.CompilerParams(vmem_limit_bytes=8 * 2**20),
         name="finish",
     )(own_grad, far_grad, weight_grad)
 
@@ -502,25 +480,25 @@
         pltpu.VMEM((4, HALF, ROWS), BF),
         pltpu.VMEM((2, ROWS, HALF), BF),
         pltpu.VMEM((4, 8, ROWS), jnp.int32),
-        pltpu.VMEM((2, ROWS, 2 * FFW), BF),
+        pltpu.VMEM((ROWS, 2 * FFW), BF),
         pltpu.VMEM((16, 16, CAP), jnp.int32),
     ]
     for shape in [(4, 4), (4,), (4,), (16, 8), (1,), (2,), (2,), (2,), (2, PARTS, 8), (PARTS,)]:
         scratch += [dma(shape), dma(shape)]
-    scratch += [dma((7,)), dma((4,)), dma((16,)), dma((2, PARTS)), dma((PARTS,)), dma((4,))]
+    scratch += [dma((6,)), dma((4,)), dma((16,)), dma((2, PARTS)), dma((4,))]
     own_grad, far_grad, weight_grad, _ = pl.pallas_call(
         kernel,
         out_shape=(
-            jax.ShapeDtypeStruct((ROWS, 2 * FFW), BF),
-            jax.ShapeDtypeStruct((ROWS, 2 * FFW), BF),
-            jax.ShapeDtypeStruct((1, FFW, FEAT), BF),
+            pltpu.VMEM((ROWS, 2 * FFW), BF),
+            pltpu.VMEM((ROWS, 2 * FFW), BF),
+            pltpu.VMEM((1, FFW, FEAT), BF),
             jax.ShapeDtypeStruct((2, FFW, FEAT), BF),
         ),
         in_specs=[hbm, vmem, hbm, hbm, hbm],
-        out_specs=(hbm, hbm, hbm, hbm),
+        out_specs=(vmem, vmem, vmem, hbm),
         scratch_shapes=scratch,
         compiler_params=pltpu.CompilerParams(
-            collective_id=0, has_side_effects=True, vmem_limit_bytes=60 * 2**20
+            collective_id=0, has_side_effects=True, vmem_limit_bytes=58 * 2**20
         ),
         name="expert_backward",
     )(out_grad, expert_ids.reshape(1, ROWS), stash_codes, jnp.swapaxes(stash_scale, 3, 4), down_weight)

time: 173 us -> 171 us (0.988)
  Pallas kernels: 173 us -> 170 us
where the time goes in v6:
time: 171 us
  Pallas kernels  170 us (99%)
    pallas_call x1, Pallas kernels, shards(): pl.pallas_call(kernel, out_shape=(pltpu.VMEM((ROWS, 2 * FFW), BF), pltpu....  169 us

profile of v6, /device:TPU:1, one launch (start us, length us, event | category | flops | bytes accessed | tf_op | source)
XLA Modules:
  0.0 171.1 jit_solution(12546276127866676631)
XLA Ops:
  0.6 168.7 %expert_backward.1 = (bf16[256,2048]{1,0:T(8,128)(2,1)S(1)}, bf16[256,2048]{1,0:T(8,128)(2,1)S(1)}, bf16[1,1024,896]{2,1,0:T(8,128)(2,1)S(1)}, bf16[2,1024,896]{2,1,0:T(8,128)(2,1)}) custom-call(bf16[256,7168]{1,0:T(8,128)(2,1)} %grad.1, s32[1,256]{1,0:T(1,128)} %bitcast.3, bf16[1,1,16,48,2048]{4,3,2,1,0:T(8,128)(2,1)} %stash.1, ...), custom_call_target="tpu_custom_call" | custom-call | tf_op jit(solution)/shard_map/expert_backward/pallas_call | solution.py:489
  169.3 1.6 finish.1

commit v7 on v6

--- a/solution.py
+++ b/solution.py
@@ -369,12 +369,12 @@
     dispatch(2, g)
     weight_copies[0].wait_recv()
     weight_copies[2].wait_recv()
+    dispatch(1, o)
     d_hidden_all(a, False)
     own_weight.wait()
     d_hidden(3, g)
     d_hidden(3, o)
     exchange(1)
-    dispatch(1, o)
     dispatch(2, o)
     dispatch(0, o)
     weight_copies[0].wait_send()

time: 171 us -> 168 us (0.982)
  Pallas kernels: 170 us -> 167 us
    pallas_call x1, Pallas kernels: 169 us -> 165 us  [shards(): pl.pallas_call(kernel, out_shape=(pltpu.VMEM((ROWS, 2 * FFW), BF), pltpu....]
where the time goes in v7:
time: 168 us
  Pallas kernels  167 us (99%)
    pallas_call x1, Pallas kernels, shards(): pl.pallas_call(kernel, out_shape=(pltpu.VMEM((ROWS, 2 * FFW), BF), pltpu....  165 us

profile of v7, /device:TPU:1, one launch (start us, length us, event | category | flops | bytes accessed | tf_op | source)
XLA Modules:
  0.0 167.7 jit_solution(8868066315688990334)
XLA Ops:
  0.6 165.3 %expert_backward.1 = (bf16[256,2048]{1,0:T(8,128)(2,1)S(1)}, bf16[256,2048]{1,0:T(8,128)(2,1)S(1)}, bf16[1,1024,896]{2,1,0:T(8,128)(2,1)S(1)}, bf16[2,1024,896]{2,1,0:T(8,128)(2,1)}) custom-call(bf16[256,7168]{1,0:T(8,128)(2,1)} %grad.1, s32[1,256]{1,0:T(1,128)} %bitcast.3, bf16[1,1,16,48,2048]{4,3,2,1,0:T(8,128)(2,1)} %stash.1, ...), custom_call_target="tpu_custom_call" | custom-call | tf_op jit(solution)/shard_map/expert_backward/pallas_call | solution.py:489
  165.9 1.6 finish.1

commit v8 on v7

--- a/solution.py
+++ b/solution.py
@@ -361,9 +361,9 @@
     dispatch(3, o)
     raw_copies[1, o].start()
     arrived(a, (0, 1, 3, 2))
+    dispatch(1, g)
     hidden_copy.wait_recv()
     partial(a)
-    dispatch(1, g)
     arrived(b, (0, 1, 3, 2))
     d_hidden_all(b, True)
     dispatch(2, g)

time: 168 us -> 168 us (level)
  no operation moved by 1% of the time
where the time goes in v8:
time: 168 us
  Pallas kernels  167 us (99%)
    pallas_call x1, Pallas kernels, shards(): pl.pallas_call(kernel, out_shape=(pltpu.VMEM((ROWS, 2 * FFW), BF), pltpu....  165 us

profile of v8, /device:TPU:1, one launch (start us, length us, event | category | flops | bytes accessed | tf_op | source)
XLA Modules:
  0.0 167.7 jit_solution(9207342289739027375)
XLA Ops:
  0.6 165.3 %expert_backward.1 = (bf16[256,2048]{1,0:T(8,128)(2,1)S(1)}, bf16[256,2048]{1,0:T(8,128)(2,1)S(1)}, bf16[1,1024,896]{2,1,0:T(8,128)(2,1)S(1)}, bf16[2,1024,896]{2,1,0:T(8,128)(2,1)}) custom-call(bf16[256,7168]{1,0:T(8,128)(2,1)} %grad.1, s32[1,256]{1,0:T(1,128)} %bitcast.3, bf16[1,1,16,48,2048]{4,3,2,1,0:T(8,128)(2,1)} %stash.1, ...), custom_call_target="tpu_custom_call" | custom-call | tf_op jit(solution)/shard_map/expert_backward/pallas_call | solution.py:489
  165.9 1.6 finish.1
